TPU v7x, 128 devices: a whole 4x4x4 slice. The times are simulated.
128 devices in a mesh: dom: 32 (over y, x, core), rep: 4 (over z).
Axes of the slice: x: 4, y: 4, z: 4, core: 2. Of those that a mesh axis runs over, the one named last changes fastest.
Arguments:
- features: bfloat16 [4, 65536, 512], P('rep', 'dom'), may hold values from -6 to 6
- w_self: bfloat16 [512, 512], replicated, may hold values from -0.25 to 0.25
- w_neigh: bfloat16 [512, 512], replicated, may hold values from -1 to 1
- out_bias: float32 [512], replicated, may hold values from -3 to 3
- cluster_plan: int32 [512], P('dom'), may hold values from 0 to 511, as said below
- local_source: int32 [512, 3], P('dom'), may hold values from 0 to 15
- halo_owner: int32 [512, 2], P('dom'), may hold values from 0 to 31, all different within a row; in each aligned block of 16 rows (0 to 15, 16 to 31, ...) at most 2 rows name the same one
- halo_local: int32 [512, 2], P('dom'), may hold values from 0 to 15
- adjacency: bfloat16 [512, 5, 128, 128], P('dom'), may hold values from 0 to 1, as said below
- cotangent: bfloat16 [4, 65536, 512], P('rep', 'dom'), may hold values from -6 to 6
Outputs:
- new_features: bfloat16 [4, 65536, 512], P('rep', 'dom')
- feature_grad: bfloat16 [4, 65536, 512], P('rep', 'dom')
- w_self_grad: float32 [512, 512], replicated
- w_neigh_grad: float32 [512, 512], replicated
- bias_grad: float32 [512], replicated
Inputs may be any that keep to these rules, and one draw needn't show every extreme that they name: `cluster_plan`: cluster c has home partition c // 16. Every cluster stands in exactly one slot. The first 13 slots of every partition hold its own clusters in home order; its slot 13 + j holds the cluster of the same home index on the partition o_j positions further along dom (cyclically), with o_j nonzero and different for different j and the same for all partitions. `halo_owner`: each row names 2 different partitions; the 16 rows of one partition name one partition at most 2 times. `adjacency`: entries are 0 or 1.
All inputs are finite; a program needn't handle non-finite values.
Results may differ from a plain program's by a relative error of at most 0.0059.
Values may be sent and summed in bfloat16 or wider, within the bound.
A program may use at most 192 MiB of HBM per device.

v0:
```python
import functools
import math

import jax
import jax.numpy as jnp
from jax import lax
from jax.experimental import pallas as pl
from jax.experimental.pallas import tpu as pltpu
from jax.sharding import PartitionSpec as P

D = 512
TILE = 128
CL = 16
KL = 3
KH = 2
MIG = 3
OWN = CL - MIG
NDOM = 32
NREP = 4
HALF = TILE // 2
WIDE = TILE + HALF
FULL = WIDE + TILE
UNITS = FULL // HALF
CHUNK = 16
SIDE = 4
GROUP = 4
STEPS = CL // GROUP
ROWS = GROUP * TILE
VMEM_LIMIT = 60 * 2**20
FACTOR = 1.0 / math.sqrt(NDOM * NREP * CL * TILE)
MESH = pl.DeviceIdType.MESH
F32 = jnp.float32
BF16 = jnp.bfloat16

ANY = pl.BlockSpec(memory_space=pl.ANY)
VMEM = pl.BlockSpec(memory_space=pltpu.VMEM)
SMEM = pl.BlockSpec(memory_space=pltpu.SMEM)


def dot_tn(a, b):
    return lax.dot_general(a, b, (((0,), (0,)), ((), ())), preferred_element_type=F32)


def dot_nt(a, b):
    return lax.dot_general(a, b, (((1,), (1,)), ((), ())), preferred_element_type=F32)


def dot_nn(a, b):
    return jnp.dot(a, b, preferred_element_type=F32)


ZROWS = D // NREP
CHIPS = NDOM // 2
CROWS = ZROWS // CHIPS

ORDER = [
    (1, 0), (3, 0), (0, 1), (0, 3), (1, 1), (3, 3), (1, 3), (3, 1),
    (2, 0), (0, 2), (2, 2), (1, 2), (2, 1), (3, 2), (2, 3),
]
PEERS = [(0, 0, 1)] + [(dx, dy, dc) for dx, dy in ORDER for dc in (0, 1)]
NPEER = len(PEERS)


class Place:
    def __init__(self):
        self.me, self.rep = lax.axis_index("dom"), lax.axis_index("rep")
        self.core, self.chip = lax.rem(self.me, 2), self.me // 2
        self.x, self.y = lax.rem(self.chip, SIDE), self.chip // SIDE
        self.partner = self.chip * 2 + 1 - self.core

    def at(self, dx, dy, dc):
        x, y = lax.rem(self.x + dx, SIDE), lax.rem(self.y + dy, SIDE)
        return (y * SIDE + x) * 2 + lax.rem(self.core + dc, 2)


def loop(low, high, f):
    def step(t, carry):
        f(t)
        return carry

    lax.fori_loop(low, high, step, 0)


def greet_plane(here, barrier):
    def one(t):
        dom = lax.rem(here.me + t, NDOM)
        pl.semaphore_signal(barrier, inc=1, device_id=(dom, here.rep), device_id_type=MESH)

    loop(1, NDOM, one)


def remote(src, dst, send_sem, recv_sem, dom, z):
    return pltpu.make_async_remote_copy(
        src_ref=src,
        dst_ref=dst,
        send_sem=send_sem,
        recv_sem=recv_sem,
        device_id=(dom, z),
        device_id_type=MESH,
    )


class Exchange:
    def __init__(self, here, src, dst, send_sem, recv_sem, first, last):
        self.here, self.src, self.dst = here, src, dst
        self.send_sem, self.recv_sem = send_sem, recv_sem
        self.first, self.last = first, last

    def copy(self, n, rows):
        dom = self.here.at(*PEERS[n])
        return remote(
            self.src.at[dom, rows],
            self.dst.at[self.here.me, rows],
            self.send_sem.at[n],
            self.recv_sem.at[n],
            dom,
            self.here.rep,
        )

    def start(self, low, high):
        def chunk(c):
            rows = pl.ds(pl.multiple_of(self.first + c * CHUNK, CHUNK), CHUNK)
            for n in range(NPEER):
                self.copy(n, rows).start()

        loop(low, high, chunk)

    def every(self, n):
        return self.copy(n, pl.ds(self.first, self.last - self.first))


def scalar_sum(terms):
    total = jnp.int32(0)
    for term in terms:
        total = total + term
    return total


class Ring:
    def __init__(self, here, steps, axis, sign, room, buffers, sems):
        self.here, self.axis, self.room, self.sems = here, axis, room, sems
        self.steps = steps if sign > 0 else [lax.rem(SIDE - s, SIDE) for s in steps]
        self.up_to, self.down_to = (SIDE - 1, 1) if sign > 0 else (1, SIDE - 1)
        self.own, self.out, self.near, self.again, self.far = buffers

    def peer(self, t):
        return self.here.at(t, 0, 0) if self.axis == "x" else self.here.at(0, t, 0)

    def ranked(self, chosen):
        rank = [scalar_sum(chosen[:j]) for j in range(MIG)]
        held = [
            scalar_sum(j * chosen[j] * (rank[j] == k).astype(jnp.int32) for j in range(MIG))
            for k in range(self.room)
        ]
        return rank, held

    def plan(self):
        up = [((s == 1) | (s == 2)).astype(jnp.int32) for s in self.steps]
        down = [(s == 3).astype(jnp.int32) for s in self.steps]
        twice = [(s == 2).astype(jnp.int32) for s in self.steps]
        return self.ranked(up), self.ranked(down), self.ranked(twice), up, down, twice

    def copies(self, n):
        room, rep = self.room, self.here.rep
        if n == 2:
            src, dst, to = self.again, self.far, self.up_to
        else:
            src = self.out.at[pl.ds(n * room, room)]
            dst = self.near.at[pl.ds(MIG + n * room, room)]
            to = (self.up_to, self.down_to)[n]
        return remote(src, dst, self.sems.at[0, n], self.sems.at[1, n], self.peer(to), rep)

    def first(self):
        (_, up_held), (_, down_held), _, _, _, _ = self.plan()
        for k in range(self.room):
            self.out[k] = self.own[up_held[k]]
            self.out[self.room + k] = self.own[down_held[k]]
        self.near[pl.ds(0, MIG)] = self.own[...]
        self.copies(0).start()
        self.copies(1).start()

    def second(self):
        (up_rank, _), _, (_, twice_held), _, _, _ = self.plan()
        self.copies(0).wait()
        self.copies(1).wait()
        for k in range(self.room):
            slot = scalar_sum(
                up_rank[j] * (twice_held[k] == j).astype(jnp.int32) for j in range(MIG)
            )
            self.again[k] = self.near[MIG + jnp.minimum(slot, self.room - 1)]
        self.copies(2).start()

    def finish(self):
        self.copies(2).wait()

    def result(self, j):
        (up_rank, _), (down_rank, _), (twice_rank, _), up, down, twice = self.plan()
        at = j + up[j] * (MIG + up_rank[j] - j) + down[j] * (MIG + self.room + down_rank[j] - j)
        late = self.far[jnp.minimum(twice_rank[j], self.room - 1)]
        soon = self.near[jnp.minimum(at, MIG + 2 * self.room - 1)]
        return jnp.where(twice[j] == 1, late, soon)


class Shift:
    def __init__(self, here, plan_ref, sign, room, scratch):
        self.here = here
        ring_x, ring_y, self.lanes, self.sems = scratch[:5], scratch[5:10], scratch[10], scratch[11]
        along_x, along_y, self.swaps = [], [], []
        for j in range(MIG):
            offset = lax.rem(plan_ref[OWN + j] // CL - here.me + NDOM, NDOM)
            if sign < 0:
                offset = lax.rem(NDOM - offset, NDOM)
            swap = lax.rem(offset, 2)
            to = lax.rem(here.core + swap, 2)
            shift = offset // 2 + to * swap
            carry = (here.x + lax.rem(shift, SIDE)) // SIDE
            along_x.append(lax.rem(shift, SIDE))
            along_y.append(lax.rem(shift // SIDE + carry, SIDE))
            self.swaps.append(swap)
        self.x = Ring(here, along_x, "x", sign, room, ring_x, self.sems.at[0])
        self.y = Ring(here, along_y, "y", sign, room, ring_y, self.sems.at[1])

    def copy_lane(self):
        slot = self.lanes.at[self.here.core]
        send_sem, recv_sem = self.sems.at[2, 0, 0], self.sems.at[2, 1, 0]
        return remote(slot, slot, send_sem, recv_sem, self.here.partner, self.here.rep)

    def turn(self):
        self.x.finish()
        for j in range(MIG):
            self.y.own[j] = self.x.result(j)
        self.y.first()

    def start_lane(self):
        self.y.finish()
        for j in range(MIG):
            self.lanes[self.here.core, j] = self.y.result(j)
        self.copy_lane().start()

    def finish(self, out_ref):
        self.copy_lane().wait()
        for j in range(MIG):
            out_ref[j] = self.lanes[lax.rem(self.here.core + self.swaps[j], 2), j]


def shift_scratch(room):
    ring = [
        pltpu.VMEM((MIG, TILE, D), BF16),
        pltpu.VMEM((2 * room, TILE, D), BF16),
        pltpu.VMEM((MIG + 2 * room, TILE, D), BF16),
        pltpu.VMEM((room, TILE, D), BF16),
        pltpu.VMEM((room, TILE, D), BF16),
    ]
    return ring + ring + [
        pltpu.VMEM((2, MIG, TILE, D), BF16),
        pltpu.SemaphoreType.DMA((3, 2, 3)),
    ]


SHIFT_REFS = 12


def few_ways(offset):
    fits = jnp.bool_(True)
    for sign, signed in ((1, offset), (-1, (NDOM - offset) % NDOM)):
        swap = signed % 2
        for core in range(2):
            shift = signed // 2 + ((core + swap) % 2) * swap
            for x in range(SIDE):
                along_x = shift % SIDE
                along_y = (shift // SIDE + (x + along_x) // SIDE) % SIDE
                for steps in (along_x, along_y):
                    steps = steps if sign > 0 else (SIDE - steps) % SIDE
                    up = jnp.sum(((steps == 1) | (steps == 2)).astype(jnp.int32))
                    down = jnp.sum((steps == 3).astype(jnp.int32))
                    fits = fits & (up <= 2) & (down <= 2)
    return fits


EXCHANGE_SEMS = pltpu.SemaphoreType.DMA((2, NPEER))


def forward_kernel(room, plan_ref, row_ref, home_ref, recv_ref, table_ref, moved_ref, *scratch):
    feat, stage, asked, table_sems, tile_sems, local_sems = scratch[:6]
    here = Place()
    me, core, rep = here.me, here.core, here.rep
    barrier = pltpu.get_barrier_semaphore()
    greet_plane(here, barrier)
    own = feat.at[pl.ds(core * CL, CL)]
    take = pltpu.make_async_copy(home_ref, own, local_sems.at[0])
    take.start()
    shift = Shift(here, plan_ref, 1, room, scratch[6:])
    mine = pltpu.make_async_copy(home_ref.at[pl.ds(OWN, MIG)], shift.x.own, local_sems.at[1])
    mine.start()
    table_ref[me] = row_ref[...]
    pl.semaphore_wait(barrier, NDOM - 1)

    def table(n):
        return remote(
            row_ref, table_ref.at[me], table_sems.at[0, n], table_sems.at[1, n],
            lax.rem(me + n, NDOM), rep,
        )

    loop(1, NDOM, lambda n: table(n).start())
    share = remote(home_ref, own, local_sems.at[2], local_sems.at[3], here.partner, rep)
    share.start()
    mine.wait()
    shift.x.first()
    loop(1, NDOM, lambda n: table(n).wait())
    read = pltpu.make_async_copy(table_ref, asked, local_sems.at[4])
    read.start()
    read.wait()
    take.wait()
    share.wait()

    def gather(p):
        first = asked[p, 0, me]
        other = asked[p, 0, NDOM + here.chip]
        stage[p, pl.ds(0, TILE)] = feat[core * CL + jnp.maximum(first, 0)]
        stage[p, pl.ds(TILE, HALF)] = feat[
            jnp.maximum(other, 0), pl.ds(pl.multiple_of(core * HALF, HALF), HALF)
        ]

    loop(0, NDOM, gather)
    keep = pltpu.make_async_copy(
        stage.at[me], recv_ref.at[me, pl.ds(0, WIDE)], local_sems.at[5]
    )
    keep.start()
    tiles = Exchange(here, stage, recv_ref, tile_sems.at[0], tile_sems.at[1], 0, WIDE)
    tiles.start(0, 2)
    shift.x.second()
    tiles.start(2, 4)
    shift.turn()
    tiles.start(4, 6)
    shift.y.second()
    tiles.start(6, 9)
    shift.start_lane()
    tiles.start(9, WIDE // CHUNK)
    keep.wait()
    for n in range(NPEER):
        tiles.every(n).wait()
    shift.finish(moved_ref)


def exchange_forward(room, plan, row, home):
    return pl.pallas_call(
        functools.partial(forward_kernel, room),
        out_shape=[
            jax.ShapeDtypeStruct((NDOM, FULL, D), BF16),
            jax.ShapeDtypeStruct((NDOM, 1, 128), jnp.int32),
            jax.ShapeDtypeStruct((MIG, TILE, D), BF16),
        ],
        in_specs=[SMEM, VMEM, ANY],
        out_specs=[ANY, VMEM, VMEM],
        scratch_shapes=[
            pltpu.VMEM((2 * CL, TILE, D), BF16),
            pltpu.VMEM((NDOM, WIDE, D), BF16),
            pltpu.SMEM((NDOM, 1, 128), jnp.int32),
            pltpu.SemaphoreType.DMA((2, NDOM)),
            EXCHANGE_SEMS,
            pltpu.SemaphoreType.DMA((6,)),
        ]
        + shift_scratch(room),
        compiler_params=pltpu.CompilerParams(
            collective_id=room - 2, has_side_effects=True, vmem_limit_bytes=VMEM_LIMIT
        ),
    )(plan, row, home)


NEAR = CL * KL


def backward_kernel(
    room, plan_ref, order_ref, back_ref, tail_ref, gp_ref, gm_ref, mean_ref, home_ref, moved_in,
    adj_ref, w_ref, ret_ref, passed_ref, moved_ref, acc_ref, out_ref, bias_ref, *scratch
):
    r1, b1, s1, r2, b2, s2, r3, b3, sums, half_sems, tile_sems, pass_sems, local_sems = scratch[:13]
    gp, gm, mean, own, adj, w, dw, db, acc, running = scratch[13:23]
    here = Place()
    me, core, chip, rep, partner = here.me, here.core, here.chip, here.rep, here.partner
    barrier = pltpu.get_barrier_semaphore()

    def z_peer(t):
        return lax.rem(rep + t, NREP)

    def chip_peer(t):
        return lax.rem(chip + t, CHIPS)

    def greet_z(t):
        pl.semaphore_signal(barrier, inc=1, device_id=(me, z_peer(t)), device_id_type=MESH)

    greet_plane(here, barrier)
    loop(1, NREP, greet_z)
    keep = pltpu.make_async_copy(
        back_ref.at[me, pl.ds(0, WIDE)], ret_ref.at[me], local_sems.at[0]
    )
    keep.start()
    loads = [
        pltpu.make_async_copy(src, dst, local_sems.at[1 + n])
        for n, (src, dst) in enumerate(
            [
                (gp_ref, gp),
                (home_ref.at[pl.ds(0, OWN)], own.at[pl.ds(0, OWN)]),
                (moved_in, own.at[pl.ds(OWN, MIG)]),
                (mean_ref, mean),
                (gm_ref, gm),
                (w_ref, w),
                (adj_ref, adj),
            ]
        )
    ]
    for copy in loads:
        copy.start()
    shift = Shift(here, plan_ref, -1, room, scratch[23:])
    shift.x.own[...] = tail_ref[...]
    pl.semaphore_wait(barrier, NDOM - 1 + NREP - 1)

    def send(src, dst, n, dom, z):
        return remote(src, dst, sums.at[0, n], sums.at[1, n], dom, z)

    halves = Exchange(here, back_ref, ret_ref, half_sems.at[0], half_sems.at[1], TILE, WIDE)
    tiles = Exchange(here, back_ref, ret_ref, tile_sems.at[0], tile_sems.at[1], 0, TILE)
    shift.x.first()
    halves.start(0, 2)

    dw[...] = jnp.zeros_like(dw)
    db[...] = jnp.zeros_like(db)
    for copy in loads[:4]:
        copy.wait()

    def weights(g):
        rows = pl.ds(g * GROUP, GROUP)
        grad = gp[rows].reshape(ROWS, D)
        dw[0] += dot_tn(own[rows].reshape(ROWS, D), grad)
        dw[1] += dot_tn(mean[rows].reshape(ROWS, D), grad)
        db[...] += jnp.sum(grad.astype(F32).reshape(ROWS // 8, 8, D), axis=0)

    loop(0, STEPS, weights)

    c_dw = send(dw.at[1 - core], r1, 0, partner, rep)
    c_db = send(db, b1, 1, partner, rep)
    c_dw.start()
    c_db.start()
    halves.start(2, 3)
    shift.x.second()
    halves.start(3, 4)
    c_db.wait()
    c_dw.wait()
    s1[...] = dw[core] + r1[...]
    b2[rep] = db[...] + b1[...]

    def z_dw(t):
        z = z_peer(t)
        return send(s1.at[pl.ds(z * ZROWS, ZROWS)], r2.at[rep], 2 + t, me, z)

    def z_db(t):
        return send(b2.at[rep], b2.at[rep], 6 + t, me, z_peer(t))

    loop(1, NREP, lambda t: z_dw(t).start())
    loop(1, NREP, lambda t: z_db(t).start())
    r2[rep] = s1[pl.ds(pl.multiple_of(rep * ZROWS, ZROWS), ZROWS)]
    shift.turn()
    tiles.start(0, 2)

    for copy in loads[4:]:
        copy.wait()

    def kept(g):
        rows = pl.ds(g * GROUP, GROUP)
        part = dot_nt(gp[rows].reshape(ROWS, D), w[...]) + gm[rows].reshape(ROWS, D).astype(F32)
        acc[rows] = part.astype(BF16).astype(F32).reshape(GROUP, TILE, D)

    loop(0, STEPS, kept)
    acc[pl.ds(OWN, MIG)] = jnp.zeros((MIG, TILE, D), F32)

    loop(1, NREP, lambda t: z_db(t).wait())
    loop(1, NREP, lambda t: z_dw(t).wait())
    s2[...] = (r2[0] + r2[1]) + (r2[2] + r2[3])
    b3[chip] = (b2[0] + b2[1]) + (b2[2] + b2[3])

    def p_dw(t):
        q = chip_peer(t)
        return send(s2.at[pl.ds(q * CROWS, CROWS)], r3.at[chip], 10 + t, q * 2 + core, rep)

    def p_db(t):
        return send(b3.at[chip], b3.at[chip], 26 + t, chip_peer(t) * 2 + core, rep)

    loop(1, CHIPS, lambda t: p_dw(t).start())
    loop(1, CHIPS, lambda t: p_db(t).start())
    r3[chip] = s2[pl.ds(pl.multiple_of(chip * CROWS, CROWS), CROWS)]
    shift.y.second()
    tiles.start(2, 4)

    running[0] = jnp.zeros((TILE, D), F32)

    def near(n):
        e = order_ref[n]
        part = dot_tn(adj[e // KL, e % KL], gm[e // KL]).astype(BF16)
        running[n + 1] = running[n] + part.astype(F32)

    loop(0, NEAR // 2, near)
    loop(1, CHIPS, lambda t: p_dw(t).wait())
    total = r3[0]
    for q in range(1, CHIPS):
        total = total + r3[q]
    mine = out_ref.at[core, pl.ds(pl.multiple_of(rep * ZROWS + chip * CROWS, CROWS), CROWS)]
    mine[...] = total

    def p_out(t):
        return send(mine, mine, 42 + t, chip_peer(t) * 2 + core, rep)

    loop(1, CHIPS, lambda t: p_out(t).start())
    shift.start_lane()
    tiles.start(4, 6)
    loop(NEAR // 2, NEAR, near)
    loop(1, CHIPS, lambda t: p_db(t).wait())
    bias = b3[0]
    for q in range(1, CHIPS):
        bias = bias + b3[q]
    bias_ref[...] = bias
    loop(1, CHIPS, lambda t: p_out(t).wait())
    block = out_ref.at[core, pl.ds(pl.multiple_of(rep * ZROWS, ZROWS), ZROWS)]

    def z_out(t):
        return send(block, block, 58 + t, me, z_peer(t))

    loop(1, NREP, lambda t: z_out(t).start())

    def pass_on(src, n):
        rows = pl.ds(TILE, HALF)
        return remote(
            ret_ref.at[src, rows], passed_ref.at[src], pass_sems.at[0, n], pass_sems.at[1, n],
            partner, rep,
        )

    keep.wait()
    pass_on(me, NPEER).start()
    for n, (dx, dy, dc) in enumerate(PEERS):
        halves.every(n).wait()
        pass_on(here.at(SIDE - dx, SIDE - dy, dc), n).start()
    tiles.start(6, TILE // CHUNK)

    def settle(h):
        acc[h] += running[order_ref[NEAR + h + 1]] - running[order_ref[NEAR + h]]

    loop(0, CL, settle)
    store = pltpu.make_async_copy(acc, acc_ref, local_sems.at[8])
    store.start()
    shift.finish(moved_ref)
    loop(1, NREP, lambda t: z_out(t).wait())
    last = send(out_ref.at[core], out_ref.at[core], 62, partner, rep)
    last.start()
    pass_on(me, NPEER).wait()
    for n, (dx, dy, dc) in enumerate(PEERS):
        pass_on(here.at(SIDE - dx, SIDE - dy, dc), n).wait()
    for n in range(NPEER):
        tiles.every(n).wait()
    last.wait()
    store.wait()


def exchange_backward(room, plan, order, back, tail, gp, gm, mean, home, moved, adjacency, w_self):
    tiles = pltpu.VMEM((CL, TILE, D), BF16)
    return pl.pallas_call(
        functools.partial(backward_kernel, room),
        out_shape=[
            jax.ShapeDtypeStruct((NDOM, WIDE, D), BF16),
            jax.ShapeDtypeStruct((NDOM, HALF, D), BF16),
            jax.ShapeDtypeStruct((MIG, TILE, D), BF16),
            jax.ShapeDtypeStruct((CL, TILE, D), F32),
            jax.ShapeDtypeStruct((2, D, D), F32),
            jax.ShapeDtypeStruct((8, D), F32),
        ],
        in_specs=[SMEM, SMEM, ANY, VMEM] + [ANY] * 7,
        out_specs=[ANY, ANY, VMEM, ANY, VMEM, VMEM],
        scratch_shapes=[
            pltpu.VMEM((D, D), F32),
            pltpu.VMEM((8, D), F32),
            pltpu.VMEM((D, D), F32),
            pltpu.VMEM((NREP, ZROWS, D), F32),
            pltpu.VMEM((NREP, 8, D), F32),
            pltpu.VMEM((ZROWS, D), F32),
            pltpu.VMEM((CHIPS, CROWS, D), F32),
            pltpu.VMEM((CHIPS, 8, D), F32),
            pltpu.SemaphoreType.DMA((2, 64)),
            EXCHANGE_SEMS,
            EXCHANGE_SEMS,
            pltpu.SemaphoreType.DMA((2, NDOM)),
            pltpu.SemaphoreType.DMA((9,)),
            tiles,
            tiles,
            tiles,
            tiles,
            pltpu.VMEM((CL, KL + KH, TILE, TILE), BF16),
            pltpu.VMEM((D, D), BF16),
            pltpu.VMEM((2, D, D), F32),
            pltpu.VMEM((8, D), F32),
            pltpu.VMEM((CL, TILE, D), F32),
            pltpu.VMEM((NEAR + 1, TILE, D), F32),
        ]
        + shift_scratch(room),
        compiler_params=pltpu.CompilerParams(
            collective_id=room, has_side_effects=True, vmem_limit_bytes=VMEM_LIMIT
        ),
    )(plan, order, back, tail, gp, gm, mean, home, moved, adjacency, w_self)


def fourth_pass(back, want_ref, home_ref, buffer_ref, out_ref, stage, sems, local_sem):
    here = Place()
    me, core = here.me, here.core
    barrier = pltpu.get_barrier_semaphore()

    def peers(which):
        return [n for n in range(NPEER) if (which + PEERS[n][2]) % 2 == 1]

    every = list(range(NPEER))
    roles = []
    for which in range(2):
        served, near = every if which == 1 else [], peers(which)
        roles.append((near, served) if back else (served, near))

    for which, (_, receives) in enumerate(roles):

        @pl.when(core == which)
        def _():
            for n in receives:
                dom = here.at(SIDE - PEERS[n][0], SIDE - PEERS[n][1], PEERS[n][2])
                pl.semaphore_signal(
                    barrier, inc=1, device_id=(dom, here.rep), device_id_type=MESH
                )

    rows = pl.ds(WIDE, TILE)
    if back:
        keep = pltpu.make_async_copy(buffer_ref.at[me, rows], out_ref.at[me], local_sem.at[0])
    else:

        def gather(p):
            stage[p] = home_ref[jnp.maximum(want_ref[p], 0)]

        loop(0, NDOM, gather)
        keep = pltpu.make_async_copy(stage.at[me], out_ref.at[me, rows], local_sem.at[0])
    keep.start()

    def copy(n, low, count):
        dom = here.at(*PEERS[n])
        if back:
            src = buffer_ref.at[dom, pl.ds(WIDE + low, count)]
            dst = out_ref.at[me, pl.ds(low, count)]
        else:
            src = stage.at[dom, pl.ds(low, count)]
            dst = out_ref.at[me, pl.ds(WIDE + low, count)]
        return remote(src, dst, sems.at[0, n], sems.at[1, n], dom, here.rep)

    def run(sends, receives):
        def chunk(c):
            for n in sends:
                copy(n, pl.multiple_of(c * CHUNK, CHUNK), CHUNK).start()

        if sends:
            pl.semaphore_wait(barrier, len(sends))
            loop(0, TILE // CHUNK, chunk)
        for n in sends:
            copy(n, 0, TILE).wait_send()
        for n in receives:
            copy(n, 0, TILE).wait_recv()

    for which, (sends, receives) in enumerate(roles):

        @pl.when(core == which)
        def _():
            run(sends, receives)

    keep.wait()


def fourth_forward(want, home, recv):
    return pl.pallas_call(
        functools.partial(fourth_pass, False),
        out_shape=jax.ShapeDtypeStruct((NDOM, FULL, D), BF16),
        in_specs=[SMEM, VMEM, ANY],
        out_specs=ANY,
        input_output_aliases={2: 0},
        scratch_shapes=[
            pltpu.VMEM((NDOM, TILE, D), BF16),
            pltpu.SemaphoreType.DMA((2, NPEER)),
            pltpu.SemaphoreType.DMA((1,)),
        ],
        compiler_params=pltpu.CompilerParams(
            collective_id=4, has_side_effects=True, vmem_limit_bytes=VMEM_LIMIT
        ),
    )(want, home, recv)


def fourth_backward(back):
    def kernel(back_ref, out_ref, sems, local_sem):
        fourth_pass(True, None, None, back_ref, out_ref, None, sems, local_sem)

    return pl.pallas_call(
        kernel,
        out_shape=jax.ShapeDtypeStruct((NDOM, TILE, D), BF16),
        in_specs=[ANY],
        out_specs=ANY,
        scratch_shapes=[pltpu.SemaphoreType.DMA((2, NPEER)), pltpu.SemaphoreType.DMA((1,))],
        compiler_params=pltpu.CompilerParams(
            collective_id=5, has_side_effects=True, vmem_limit_bytes=VMEM_LIMIT
        ),
    )(back)


def tile_block(width=D):
    return pl.BlockSpec((GROUP, TILE, width), lambda g, *_: (g, 0, 0))


def whole(*shape):
    return pl.BlockSpec(shape, lambda g, *_: (0,) * len(shape))


def adj_block(k):
    return pl.BlockSpec((GROUP, 1, TILE, TILE), lambda g, *_: (g, k, 0, 0))


def own_tile(i, g, home_tile, moved_ref):
    j = CL - GROUP + i - OWN
    if j < 0:
        return home_tile
    return jnp.where(g == STEPS - 1, moved_ref[j], home_tile)


PARTS = 2 * GROUP * KH


def middle_kernel(block_ref, src_ref, *refs):
    halo = refs[:PARTS]
    (home_ref, moved_ref, adj_ref, cot_ref, ws_ref, wn_ref, bias_ref) = refs[PARTS : PARTS + 7]
    (new_ref, gp_ref, mean_ref, gm_ref, tail_ref, back_ref) = refs[PARTS + 7 : PARTS + 13]
    (own, scale, grads, sem) = refs[PARTS + 13 :]
    g = pl.program_id(0)
    for i in range(GROUP):
        slot = g * GROUP + i
        rows = pl.ds(i * TILE, TILE)
        mine = own_tile(i, g, home_ref[slot], moved_ref)
        own[rows] = mine
        adj = jnp.concatenate([adj_ref[i, k] for k in range(KL + KH)], axis=1)
        total = jnp.sum(adj.astype(F32), axis=1, keepdims=True)
        scale[rows] = jnp.broadcast_to(1.0 / (1.0 + total), (TILE, D))
        near = [home_ref[src_ref[slot * KL + k]] for k in range(KL)]
        far = [halo[2 * KH * i + n][0] for n in range(2 * KH)]
        agg = mine.astype(F32) + dot_nn(adj, jnp.concatenate(near + far, axis=0))
        mean_ref[i] = (agg * scale[rows]).astype(BF16)
    pre = (
        dot_nn(own[...], ws_ref[...])
        + dot_nn(mean_ref[...].reshape(ROWS, D), wn_ref[...])
        + bias_ref[...]
    )
    sig = 1.0 / (1.0 + jnp.exp(-pre))
    new_ref[...] = (pre * sig).astype(BF16).reshape(GROUP, TILE, D)
    cot = cot_ref[...].reshape(ROWS, D).astype(F32)
    gp = (cot * sig * (1.0 + pre * (1.0 - sig))).astype(BF16)
    gp_ref[...] = gp.reshape(GROUP, TILE, D)
    gm = (dot_nt(gp, wn_ref[...]) * scale[...]).astype(BF16)
    gm_ref[...] = gm.reshape(GROUP, TILE, D)

    def copy(n):
        return pltpu.make_async_copy(grads.at[n], back_ref.at[block_ref[n]], sem.at[n])

    for i in range(GROUP):
        adj = jnp.concatenate([adj_ref[i, KL + k] for k in range(KH)], axis=1)
        both = dot_tn(adj, gm[i * TILE : (i + 1) * TILE]).astype(BF16)
        for part in range(2 * KH):
            n = (g * GROUP + i) * 2 * KH + part
            grads[n] = both[part * HALF : (part + 1) * HALF]
            copy(n).start()

    @pl.when(g == STEPS - 1)
    def _():
        first = TILE * (GROUP - MIG)
        tail = dot_nt(gp[first:], ws_ref[...]) + gm[first:].astype(F32)
        tail_ref[...] = tail.astype(BF16).reshape(MIG, TILE, D)
        loop(0, 2 * CL * KH, lambda n: copy(n).wait())


def middle(blocks, src, recv, home, moved, adjacency, cot, w_self, w_neigh, bias):
    def halo_block(n):
        return pl.BlockSpec((1, HALF, D), lambda g, blocks, src: (blocks[g * PARTS + n], 0, 0))

    tiles = jax.ShapeDtypeStruct((CL, TILE, D), BF16)
    return pl.pallas_call(
        middle_kernel,
        out_shape=[
            tiles, tiles, tiles, tiles,
            jax.ShapeDtypeStruct((MIG, TILE, D), BF16),
            jax.ShapeDtypeStruct(recv.shape, BF16),
        ],
        grid_spec=pltpu.PrefetchScalarGridSpec(
            num_scalar_prefetch=2,
            grid=(STEPS,),
            in_specs=[halo_block(n) for n in range(PARTS)]
            + [
                whole(CL, TILE, D),
                whole(MIG, TILE, D),
                pl.BlockSpec((GROUP, KL + KH, TILE, TILE), lambda g, *_: (g, 0, 0, 0)),
                tile_block(),
                whole(D, D),
                whole(D, D),
                whole(1, D),
            ],
            out_specs=[tile_block()] * 4 + [whole(MIG, TILE, D), ANY],
            scratch_shapes=[
                pltpu.VMEM((ROWS, D), BF16),
                pltpu.VMEM((ROWS, D), F32),
                pltpu.VMEM((2 * CL * KH, HALF, D), BF16),
                pltpu.SemaphoreType.DMA((2 * CL * KH,)),
            ],
        ),
        compiler_params=pltpu.CompilerParams(vmem_limit_bytes=VMEM_LIMIT),
    )(
        blocks, src, *([recv] * PARTS), home, moved, adjacency, cot, w_self, w_neigh, bias
    )


FOUR = 4


def final_kernel(first_ref, other_ref, more_ref, acc_ref, moved_ref, back_ref, passed_ref, *refs):
    extra_ref = refs[0] if len(refs) == 8 else None
    dw_ref, db_ref, out_ref, dws_ref, dwn_ref, bias_ref, acc = refs[-7:]
    g = pl.program_id(0)
    here_half = lax.rem(lax.axis_index("dom"), 2)
    dws_ref[...] = dw_ref[0] * FACTOR
    dwn_ref[...] = dw_ref[1] * FACTOR

    @pl.when(g == 0)
    def _():
        bias_ref[...] = jnp.sum(db_ref[...], axis=0, keepdims=True) * FACTOR
        acc[...] = acc_ref[...]
        for j in range(MIG):
            acc[OWN + j] += moved_ref[j].astype(F32)

    for n in range(FOUR):
        c = g * FOUR + n
        first, other = first_ref[c], other_ref[c]

        @pl.when(first >= 0)
        def _():
            acc[first] += back_ref[n, pl.ds(0, TILE)].astype(F32)

        @pl.when(other >= 0)
        def _():
            rows = pl.ds(pl.multiple_of(here_half * HALF, HALF), HALF)
            acc[other, rows] += back_ref[n, pl.ds(TILE, HALF)].astype(F32)
            rows = pl.ds(pl.multiple_of((1 - here_half) * HALF, HALF), HALF)
            acc[other, rows] += passed_ref[n].astype(F32)

        if extra_ref is not None:
            more = more_ref[c]

            @pl.when(more >= 0)
            def _():
                acc[more] += extra_ref[n].astype(F32)

    @pl.when(g == NDOM // FOUR - 1)
    def _():
        out_ref[...] = acc[...].astype(BF16)


def finish(first, other, more, acc, moved, back, passed, extra, dw, db):
    steps = NDOM // FOUR

    def four(rows):
        return pl.BlockSpec((FOUR, rows, D), lambda g, *_: (g, 0, 0))

    extras = [] if extra is None else [extra]
    return pl.pallas_call(
        final_kernel,
        out_shape=[
            jax.ShapeDtypeStruct((CL, TILE, D), BF16),
            jax.ShapeDtypeStruct((D, D), F32),
            jax.ShapeDtypeStruct((D, D), F32),
            jax.ShapeDtypeStruct((1, D), F32),
        ],
        grid_spec=pltpu.PrefetchScalarGridSpec(
            num_scalar_prefetch=3,
            grid=(steps,),
            in_specs=[whole(CL, TILE, D), whole(MIG, TILE, D), four(WIDE), four(HALF)]
            + [four(TILE)] * len(extras)
            + [pl.BlockSpec((2, D // steps, D), lambda g, *_: (0, g, 0)), whole(8, D)],
            out_specs=[whole(CL, TILE, D)]
            + [pl.BlockSpec((D // steps, D), lambda g, *_: (g, 0))] * 2
            + [whole(1, D)],
            scratch_shapes=[pltpu.VMEM((CL, TILE, D), F32)],
        ),
        compiler_params=pltpu.CompilerParams(vmem_limit_bytes=VMEM_LIMIT),
    )(first, other, more, acc, moved, back, passed, *extras, dw, db)


def requests(owner, local):
    entries = jnp.arange(owner.shape[0], dtype=jnp.int32)
    same = owner[:, None] == owner[None, :]
    second = jnp.any(same & (entries[None, :] < entries[:, None]), axis=1)
    partner = (owner[:, None] ^ 1) == owner[None, :]
    fourth = second & (owner % 2 == 1) & jnp.any(partner & second[None, :], axis=1)
    chip = owner // 2

    column = jnp.where(second, jnp.where(fourth, NDOM + CHIPS + chip, NDOM + chip), owner)
    value = jnp.where(second & ~fourth, (owner % 2) * CL + local, local)
    hit = column[:, None] == jnp.arange(128, dtype=jnp.int32)[None, :]
    row = jnp.sum(jnp.where(hit, value[:, None] + 1, 0), axis=0) - 1
    low = jnp.where(
        fourth, UNITS * owner + 3, jnp.where(second, 2 * UNITS * chip + 2, UNITS * owner)
    )
    high = jnp.where(second & ~fourth, low + UNITS, low + 1)
    return row, jnp.stack([low, high], axis=1).reshape(-1)


def sorted_near(src):
    entries = jnp.arange(NEAR, dtype=jnp.int32)
    ahead = (src[None, :] < src[:, None]) | (
        (src[None, :] == src[:, None]) & (entries[None, :] < entries[:, None])
    )
    rank = jnp.sum(ahead.astype(jnp.int32), axis=1)
    order = jnp.sum(jnp.where(rank[None, :] == entries[:, None], entries[None, :], 0), axis=1)
    begins = jnp.sum(
        (src[None, :] < jnp.arange(CL + 1, dtype=jnp.int32)[:, None]).astype(jnp.int32), axis=1
    )
    return jnp.concatenate([order, begins])


def body(
    features, w_self, w_neigh, out_bias, cluster_plan, local_source, halo_owner, halo_local,
    adjacency, cotangent,
):
    me = lax.axis_index("dom")
    core, chip = me % 2, me // 2
    home = features[0].reshape(CL, TILE, D)
    cot = cotangent[0].reshape(CL, TILE, D)
    src = local_source.reshape(-1)
    bias = out_bias.reshape(1, D)
    row, blocks = requests(halo_owner.reshape(-1), halo_local.reshape(-1))
    offset = (cluster_plan[OWN:] // CL - me + NDOM) % NDOM
    few = few_ways(offset)
    recv, tables, moved = lax.cond(
        few,
        functools.partial(exchange_forward, 2),
        functools.partial(exchange_forward, 3),
        cluster_plan,
        row.reshape(1, 128),
        home,
    )
    asked = tables[:, 0, :]
    first = lax.dynamic_slice(asked, (0, me), (NDOM, 1)).reshape(-1)
    other = lax.dynamic_slice(asked, (0, NDOM + chip), (NDOM, 1)).reshape(-1)
    more = lax.dynamic_slice(asked, (0, NDOM + CHIPS + chip), (NDOM, 1)).reshape(-1)
    other = jnp.where((other >= 0) & (other // CL == core), other % CL, -1)
    more_here = jnp.where(core == 1, more, -1)
    order = sorted_near(src)

    def rest_of(extra, room, recv, moved):
        if extra:
            recv = fourth_forward(more, home, recv)
        new, gp, mean, gm, tail, back = middle(
            blocks, src, recv.reshape(NDOM * UNITS, HALF, D), home, moved, adjacency, cot,
            w_self, w_neigh, bias,
        )
        back = back.reshape(NDOM, FULL, D)
        ret, passed, returned, acc, dw, db = exchange_backward(
            room, cluster_plan, order, back, tail, gp, gm, mean, home, moved, adjacency, w_self
        )
        got = fourth_backward(back) if extra else None
        return new, *finish(first, other, more_here, acc, returned, ret, passed, got, dw, db)

    extra = jnp.any(asked[:, NDOM + CHIPS : NDOM + 2 * CHIPS] >= 0)
    new, grad, dws, dwn, db = lax.switch(
        2 * extra.astype(jnp.int32) + 1 - few.astype(jnp.int32),
        [functools.partial(rest_of, more, room) for more in (False, True) for room in (2, 3)],
        recv,
        moved,
    )
    return (
        new.reshape(1, CL * TILE, D), grad.reshape(1, CL * TILE, D), dws, dwn, db.reshape(D)
    )


def solution(mesh):
    return jax.shard_map(
        body,
        mesh=mesh,
        in_specs=(
            P("rep", "dom", None),
            P(),
            P(),
            P(),
            P("dom"),
            P("dom", None),
            P("dom", None),
            P("dom", None),
            P("dom", None, None, None),
            P("rep", "dom", None),
        ),
        out_specs=(P("rep", "dom", None), P("rep", "dom", None), P(), P(), P()),
        check_vma=False,
    )
```

profile of v0, /device:TPU:1, one launch (start us, length us, event | category | flops | bytes accessed | tf_op | source)
XLA Modules:
  0.0 359.2 jit_solution(14893111825066858926)
XLA Ops:
  0.6 0.8 and_select_fusion.42
  1.5 0.6 and_select_fusion.56
  3.4 0.6 fusion.17
  5.3 0.6 fusion.19
  7.3 0.6 fusion.21
  9.3 0.6 fusion.23
  11.2 0.6 and_select_fusion.45
  21.1 0.6 fusion.35
  25.0 0.6 fusion.41
  30.8 0.6 fusion.49
  34.7 0.6 fusion.55
  38.7 0.6 fusion.61
  40.6 0.8 copy.27
  41.8 0.8 copy.28
  42.9 97.3 %conditional.2 = (s32[32,1,128]{2,1,0:T(1,128)S(1)}, bf16[32,320,512]{2,1,0:T(8,128)(2,1)}, bf16[3,128,512]{2,1,0:T(8,128)(2,1)S(1)}) conditional(s32[]{:T(128)} %convert_element_type.195, (s32[16]{0:T(128)}, s32[1,128]{1,0:T(1,128)S(1)}, bf16[16,128,512]{2,1,0:T(8,128)(2,1)}) %tuple.112, (s32[16]{0:T(128)}, s32[1,128]{1,0:T(1,128)S(1)}, ...), branch_computations={%region_43.44_spmd.clone, %region_44.45_spmd.clone} | conditional | bytes 24 | solution.py:941
  42.9 97.3 %branch_1_fun.8 = (bf16[32,320,512]{2,1,0:T(8,128)(2,1)}, s32[32,1,128]{2,1,0:T(1,128)S(1)}, bf16[3,128,512]{2,1,0:T(8,128)(2,1)S(1)}) custom-call(s32[16]{0:T(128)} %get-tuple-element.322.plan_ref, s32[1,128]{1,0:T(1,128)S(1)} %get-tuple-element.323.row_ref, bf16[16,128,512]{2,1,0:T(8,128)(2,1)} %get-tuple-element.324.home_ref), custom_call_target="tpu_custom_call" | custom-call | tf_op jit(solution)/shard_map/cond/branch_1_fun/pallas_call | solution.py:346
  140.2 0.7 fusion.4
  142.6 1.9 dynamic-slice_reduce_fusion
  144.6 213.3 %conditional.3 = (bf16[16,128,512]{2,1,0:T(8,128)(2,1)}, bf16[16,128,512]{2,1,0:T(8,128)(2,1)}, f32[512,512]{1,0:T(8,128)}, f32[512,512]{1,0:T(8,128)}, f32[1,512]{1,0:T(1,128)}) conditional(s32[]{:T(128)} %clamp.3, (bf16[32,320,512]{2,1,0:T(8,128)(2,1)}, s32[64]{0:T(128)S(1)}, s32[48]{0:T(128)S(1)}, ...), branch_computations={%region_49.50_spmd, %region_50.51_spmd, %region_51.52_spmd, %regio... | conditional | bytes 8388960 | solution.py:972
  152.7 32.4 %branch_2_fun.5 = bf16[32,320,512]{2,1,0:T(8,128)(2,1)} custom-call(s32[32]{0:T(128)S(1)} %get-tuple-element.230.want_ref, bf16[16,128,512]{2,1,0:T(8,128)(2,1)} %get-tuple-element.231.home_ref.refs_16_, bf16[32,320,512]{2,1,0:T(8,128)(2,1)} %get-tuple-element.232.buffer_ref), custom_call_target="tpu_custom_call", output_to_operand_aliasing={{}: (2, {})} | custom-call | tf_op jit(solution)/shard_map/cond/branch_2_fun/pallas_call | solution.py:677
  185.1 14.2 %branch_2_fun.6 = (bf16[16,128,512]{2,1,0:T(8,128)(2,1)}, bf16[16,128,512]{2,1,0:T(8,128)(2,1)}, bf16[16,128,512]{2,1,0:T(8,128)(2,1)}, bf16[16,128,512]{2,1,0:T...) custom-call(s32[64]{0:T(128)S(1)} %get-tuple-element.228.block_ref, ...), custom_call_target="tpu_custom_call" | custom-call | tf_op jit(solution)/shard_map/cond/branch_2_fun/pallas_call | solution.py:787
  199.3 116.3 %branch_2_fun.7 = (bf16[32,192,512]{2,1,0:T(8,128)(2,1)}, bf16[32,64,512]{2,1,0:T(8,128)(2,1)}, bf16[3,128,512]{2,1,0:T(8,128)(2,1)}, f32[16,128,512]{2,1,0:T(8,...) custom-call(s32[16]{0:T(128)S(1)} %copy-done.9, s32[65]{0:T(128)S(1)} %get-tuple-element.244.order_ref, ...), custom_call_target="tpu_custom_call" | custom-call | tf_op jit(solution)/shard_map/cond/branch_2_fun/pallas_call | solution.py:564
  315.6 29.6 %branch_2_fun.8.refs_0_ = bf16[32,128,512]{2,1,0:T(8,128)(2,1)} custom-call(bf16[32,320,512]{2,1,0:T(8,128)(2,1)} %bitcast.101), custom_call_target="tpu_custom_call" | custom-call | tf_op jit(solution)/shard_map/cond/branch_2_fun/pallas_call | solution.py:698
  345.2 11.7 %branch_2_fun.9 = (bf16[16,128,512]{2,1,0:T(8,128)(2,1)}, f32[512,512]{1,0:T(8,128)}, f32[512,512]{1,0:T(8,128)}, f32[1,512]{1,0:T(1,128)}) custom-call(s32[32]{0:T(128)S(1)} %get-tuple-element.240.first_ref, s32[32]{0:T(128)S(1)} %get-tuple-element.241.other_ref, s32[32]{0:T(128)S(1)} %get-tuple-element.242.more_ref, ...), custom_call_target="tpu_custom_call" | custom-call | tf_op jit(solution)/shard_map/cond/branch_2_fun/pallas_call | solution.py:873
  (48 shorter events, 7.6 us)
Async XLA Ops:
  42.8 99.1 %copy-start.11 = (s32[16,3]{0,1:T(4,128)S(1)}, s32[16,3]{0,1:T(4,128)}, u32[]{:S(2)}) copy-start(s32[16,3]{0,1:T(4,128)} %param.21) | copy-start | bytes 580
  42.8 101.7 %copy-start.4 = (bf16[512,512]{1,0:T(8,128)(2,1)S(1)}, bf16[512,512]{1,0:T(8,128)(2,1)}, u32[]{:S(2)}) copy-start(bf16[512,512]{1,0:T(8,128)(2,1)} %param.17) | copy-start | bytes 1572868
  42.8 101.7 %copy-start.5 = (bf16[512,512]{1,0:T(8,128)(2,1)S(1)}, bf16[512,512]{1,0:T(8,128)(2,1)}, u32[]{:S(2)}) copy-start(bf16[512,512]{1,0:T(8,128)(2,1)} %param.18) | copy-start | bytes 1572868
  42.8 101.7 %copy-start.6 = (f32[512]{0:T(512)S(1)}, f32[512]{0:T(512)}, u32[]{:S(2)}) copy-start(f32[512]{0:T(512)} %param.19) | copy-start | bytes 6148
  152.7 32.4 %copy-start.2 = (bf16[16,128,512]{2,1,0:T(8,128)(2,1)S(1)}, bf16[16,128,512]{2,1,0:T(8,128)(2,1)}, u32[]{:S(2)}) copy-start(bf16[16,128,512]{2,1,0:T(8,128)(2,1)} %get-tuple-element.231.home_ref.refs_16_) | copy-start | bytes 6291460 | tf_op jit(solution)/shard_map/cond
  185.1 14.3 %copy-start.9 = (s32[16]{0:T(128)S(1)}, s32[16]{0:T(128)}, u32[]{:S(2)}) copy-start(s32[16]{0:T(128)} %get-tuple-element.243.plan_ref) | copy-start | bytes 196 | tf_op jit(solution)/shard_map/cond
where the time goes:
time: 366 us; the launch traced here: 359 us
  Pallas kernels  301 us (82%)
  between operations  29.1 us (8%)
  other arithmetic  15.4 us (4%)
  loops' own time  9.08 us (2%)
  local copies, waits for them, and re-layouts  4.1 us (1%)
    pallas_call x1, Pallas kernels, exchange_backward(): pl.pallas_call(functools.partial(backward_kernel, room), out_shape=[jax.S...  116 us
    pallas_call x1, Pallas kernels, exchange_forward(): pl.pallas_call(functools.partial(forward_kernel, room), out_shape=[jax.Sh...  97.3 us
    pallas_call x1, Pallas kernels, fourth_forward(): pl.pallas_call(functools.partial(fourth_pass, False), out_shape=jax.Shape...  32.4 us
    pallas_call x1, Pallas kernels, fourth_backward(): pl.pallas_call(kernel, out_shape=jax.ShapeDtypeStruct((NDOM, TILE, D), BF...  29.6 us
    pallas_call x1, Pallas kernels, middle(): pl.pallas_call(middle_kernel, out_shape=[tiles, tiles, tiles, tiles, jax....  14.2 us
    pallas_call x1, Pallas kernels, finish(): pl.pallas_call(final_kernel, out_shape=[jax.ShapeDtypeStruct((CL, TILE, D...  11.7 us
    reduce_sum x18, other arithmetic, few_ways(): down = jnp.sum((steps == 3).astype(jnp.int32))  11.4 us
    another operation x1, loops' own time, body(): lax.switch(2 * extra.astype(jnp.int32) + 1 - few.astype(jnp.int32), [func...  9.06 us

commit v1 on v0

--- a/solution.py
+++ b/solution.py
@@ -140,71 +140,57 @@
     def __init__(self, here, steps, axis, sign, room, buffers, sems):
         self.here, self.axis, self.room, self.sems = here, axis, room, sems
         self.steps = steps if sign > 0 else [lax.rem(SIDE - s, SIDE) for s in steps]
-        self.up_to, self.down_to = (SIDE - 1, 1) if sign > 0 else (1, SIDE - 1)
-        self.own, self.out, self.near, self.again, self.far = buffers
+        self.to = (SIDE - 1, 1, 2) if sign > 0 else (1, SIDE - 1, 2)
+        self.own, self.out, self.near = buffers
 
     def peer(self, t):
         return self.here.at(t, 0, 0) if self.axis == "x" else self.here.at(0, t, 0)
 
-    def ranked(self, chosen):
-        rank = [scalar_sum(chosen[:j]) for j in range(MIG)]
-        held = [
-            scalar_sum(j * chosen[j] * (rank[j] == k).astype(jnp.int32) for j in range(MIG))
-            for k in range(self.room)
-        ]
-        return rank, held
-
-    def plan(self):
-        up = [((s == 1) | (s == 2)).astype(jnp.int32) for s in self.steps]
-        down = [(s == 3).astype(jnp.int32) for s in self.steps]
-        twice = [(s == 2).astype(jnp.int32) for s in self.steps]
-        return self.ranked(up), self.ranked(down), self.ranked(twice), up, down, twice
-
-    def copies(self, n):
-        room, rep = self.room, self.here.rep
-        if n == 2:
-            src, dst, to = self.again, self.far, self.up_to
-        else:
-            src = self.out.at[pl.ds(n * room, room)]
-            dst = self.near.at[pl.ds(MIG + n * room, room)]
-            to = (self.up_to, self.down_to)[n]
-        return remote(src, dst, self.sems.at[0, n], self.sems.at[1, n], self.peer(to), rep)
-
-    def first(self):
-        (_, up_held), (_, down_held), _, _, _, _ = self.plan()
-        for k in range(self.room):
-            self.out[k] = self.own[up_held[k]]
-            self.out[self.room + k] = self.own[down_held[k]]
+    def ways(self):
+        first = 0
+        for way, step in enumerate((1, SIDE - 1, 2)):
+            chosen = [(s == step).astype(jnp.int32) for s in self.steps]
+            rank = [scalar_sum(chosen[:j]) for j in range(MIG)]
+            yield way, first, chosen, rank
+            first += self.room[way]
+
+    def copy(self, way, first):
+        room = self.room[way]
+        return remote(
+            self.out.at[pl.ds(first, room)],
+            self.near.at[pl.ds(MIG + first, room)],
+            self.sems.at[0, way],
+            self.sems.at[1, way],
+            self.peer(self.to[way]),
+            self.here.rep,
+        )
+
+    def start(self):
+        for way, first, chosen, rank in self.ways():
+            for k in range(self.room[way]):
+                held = scalar_sum(
+                    j * chosen[j] * (rank[j] == k).astype(jnp.int32) for j in range(MIG)
+                )
+                self.out[first + k] = self.own[held]
+            self.copy(way, first).start()
         self.near[pl.ds(0, MIG)] = self.own[...]
-        self.copies(0).start()
-        self.copies(1).start()
-
-    def second(self):
-        (up_rank, _), _, (_, twice_held), _, _, _ = self.plan()
-        self.copies(0).wait()
-        self.copies(1).wait()
-        for k in range(self.room):
-            slot = scalar_sum(
-                up_rank[j] * (twice_held[k] == j).astype(jnp.int32) for j in range(MIG)
-            )
-            self.again[k] = self.near[MIG + jnp.minimum(slot, self.room - 1)]
-        self.copies(2).start()
 
     def finish(self):
-        self.copies(2).wait()
+        for way, first, _, _ in self.ways():
+            self.copy(way, first).wait()
 
     def result(self, j):
-        (up_rank, _), (down_rank, _), (twice_rank, _), up, down, twice = self.plan()
-        at = j + up[j] * (MIG + up_rank[j] - j) + down[j] * (MIG + self.room + down_rank[j] - j)
-        late = self.far[jnp.minimum(twice_rank[j], self.room - 1)]
-        soon = self.near[jnp.minimum(at, MIG + 2 * self.room - 1)]
-        return jnp.where(twice[j] == 1, late, soon)
+        at = jnp.int32(j)
+        for way, first, chosen, rank in self.ways():
+            slot = MIG + first + jnp.minimum(rank[j], self.room[way] - 1)
+            at = at + chosen[j] * (slot - j)
+        return self.near[at]
 
 
 class Shift:
     def __init__(self, here, plan_ref, sign, room, scratch):
         self.here = here
-        ring_x, ring_y, self.lanes, self.sems = scratch[:5], scratch[5:10], scratch[10], scratch[11]
+        ring_x, ring_y, self.lanes, self.sems = scratch[:3], scratch[3:6], scratch[6], scratch[7]
         along_x, along_y, self.swaps = [], [], []
         for j in range(MIG):
             offset = lax.rem(plan_ref[OWN + j] // CL - here.me + NDOM, NDOM)
@@ -229,7 +215,7 @@
         self.x.finish()
         for j in range(MIG):
             self.y.own[j] = self.x.result(j)
-        self.y.first()
+        self.y.start()
 
     def start_lane(self):
         self.y.finish()
@@ -243,13 +229,14 @@
             out_ref[j] = self.lanes[lax.rem(self.here.core + self.swaps[j], 2), j]
 
 
+ROOMS = [(1, 2, 2), (MIG, MIG, MIG)]
+
+
 def shift_scratch(room):
     ring = [
         pltpu.VMEM((MIG, TILE, D), BF16),
-        pltpu.VMEM((2 * room, TILE, D), BF16),
-        pltpu.VMEM((MIG + 2 * room, TILE, D), BF16),
-        pltpu.VMEM((room, TILE, D), BF16),
-        pltpu.VMEM((room, TILE, D), BF16),
+        pltpu.VMEM((sum(room), TILE, D), BF16),
+        pltpu.VMEM((MIG + sum(room), TILE, D), BF16),
     ]
     return ring + ring + [
         pltpu.VMEM((2, MIG, TILE, D), BF16),
@@ -257,23 +244,21 @@
     ]
 
 
-SHIFT_REFS = 12
-
-
 def few_ways(offset):
+    back = jnp.arange(2, dtype=jnp.int32)[:, None, None, None]
+    core = jnp.arange(2, dtype=jnp.int32)[None, :, None, None]
+    x = jnp.arange(SIDE, dtype=jnp.int32)[None, None, :, None]
+    signed = jnp.where(back == 1, NDOM - offset, offset)
+    swap = signed & 1
+    shift = (signed >> 1) + ((core + swap) & 1) * swap
+    along_x = shift & (SIDE - 1)
+    along_y = ((shift >> 2) + ((x + along_x) >> 2)) & (SIDE - 1)
     fits = jnp.bool_(True)
-    for sign, signed in ((1, offset), (-1, (NDOM - offset) % NDOM)):
-        swap = signed % 2
-        for core in range(2):
-            shift = signed // 2 + ((core + swap) % 2) * swap
-            for x in range(SIDE):
-                along_x = shift % SIDE
-                along_y = (shift // SIDE + (x + along_x) // SIDE) % SIDE
-                for steps in (along_x, along_y):
-                    steps = steps if sign > 0 else (SIDE - steps) % SIDE
-                    up = jnp.sum(((steps == 1) | (steps == 2)).astype(jnp.int32))
-                    down = jnp.sum((steps == 3).astype(jnp.int32))
-                    fits = fits & (up <= 2) & (down <= 2)
+    for steps in (jnp.broadcast_to(along_x, along_y.shape), along_y):
+        steps = jnp.where(back == 1, (SIDE - steps) & (SIDE - 1), steps)
+        for way, step in enumerate((1, SIDE - 1, 2)):
+            count = jnp.sum((steps == step).astype(jnp.int32), axis=-1)
+            fits = fits & jnp.all(count <= ROOMS[0][way])
     return fits
 
 
@@ -305,7 +290,7 @@
     share = remote(home_ref, own, local_sems.at[2], local_sems.at[3], here.partner, rep)
     share.start()
     mine.wait()
-    shift.x.first()
+    shift.x.start()
     loop(1, NDOM, lambda n: table(n).wait())
     read = pltpu.make_async_copy(table_ref, asked, local_sems.at[4])
     read.start()
@@ -327,15 +312,11 @@
     )
     keep.start()
     tiles = Exchange(here, stage, recv_ref, tile_sems.at[0], tile_sems.at[1], 0, WIDE)
-    tiles.start(0, 2)
-    shift.x.second()
-    tiles.start(2, 4)
+    tiles.start(0, 3)
     shift.turn()
-    tiles.start(4, 6)
-    shift.y.second()
-    tiles.start(6, 9)
+    tiles.start(3, 7)
     shift.start_lane()
-    tiles.start(9, WIDE // CHUNK)
+    tiles.start(7, WIDE // CHUNK)
     keep.wait()
     for n in range(NPEER):
         tiles.every(n).wait()
@@ -362,7 +343,7 @@
         ]
         + shift_scratch(room),
         compiler_params=pltpu.CompilerParams(
-            collective_id=room - 2, has_side_effects=True, vmem_limit_bytes=VMEM_LIMIT
+            collective_id=ROOMS.index(room), has_side_effects=True, vmem_limit_bytes=VMEM_LIMIT
         ),
     )(plan, row, home)
 
@@ -420,7 +401,7 @@
 
     halves = Exchange(here, back_ref, ret_ref, half_sems.at[0], half_sems.at[1], TILE, WIDE)
     tiles = Exchange(here, back_ref, ret_ref, tile_sems.at[0], tile_sems.at[1], 0, TILE)
-    shift.x.first()
+    shift.x.start()
     halves.start(0, 2)
 
     dw[...] = jnp.zeros_like(dw)
@@ -433,7 +414,7 @@
         grad = gp[rows].reshape(ROWS, D)
         dw[0] += dot_tn(own[rows].reshape(ROWS, D), grad)
         dw[1] += dot_tn(mean[rows].reshape(ROWS, D), grad)
-        db[...] += jnp.sum(grad.astype(F32).reshape(ROWS // 8, 8, D), axis=0)
+        db[...] += jnp.sum(grad.astype(F32), axis=0, keepdims=True)
 
     loop(0, STEPS, weights)
 
@@ -441,9 +422,7 @@
     c_db = send(db, b1, 1, partner, rep)
     c_dw.start()
     c_db.start()
-    halves.start(2, 3)
-    shift.x.second()
-    halves.start(3, 4)
+    halves.start(2, 4)
     c_db.wait()
     c_dw.wait()
     s1[...] = dw[core] + r1[...]
@@ -459,8 +438,8 @@
     loop(1, NREP, lambda t: z_dw(t).start())
     loop(1, NREP, lambda t: z_db(t).start())
     r2[rep] = s1[pl.ds(pl.multiple_of(rep * ZROWS, ZROWS), ZROWS)]
+    tiles.start(0, 2)
     shift.turn()
-    tiles.start(0, 2)
 
     for copy in loads[4:]:
         copy.wait()
@@ -488,7 +467,6 @@
     loop(1, CHIPS, lambda t: p_dw(t).start())
     loop(1, CHIPS, lambda t: p_db(t).start())
     r3[chip] = s2[pl.ds(pl.multiple_of(chip * CROWS, CROWS), CROWS)]
-    shift.y.second()
     tiles.start(2, 4)
 
     running[0] = jnp.zeros((TILE, D), F32)
@@ -569,19 +547,19 @@
             jax.ShapeDtypeStruct((MIG, TILE, D), BF16),
             jax.ShapeDtypeStruct((CL, TILE, D), F32),
             jax.ShapeDtypeStruct((2, D, D), F32),
-            jax.ShapeDtypeStruct((8, D), F32),
+            jax.ShapeDtypeStruct((1, D), F32),
         ],
         in_specs=[SMEM, SMEM, ANY, VMEM] + [ANY] * 7,
         out_specs=[ANY, ANY, VMEM, ANY, VMEM, VMEM],
         scratch_shapes=[
             pltpu.VMEM((D, D), F32),
-            pltpu.VMEM((8, D), F32),
+            pltpu.VMEM((1, D), F32),
             pltpu.VMEM((D, D), F32),
             pltpu.VMEM((NREP, ZROWS, D), F32),
-            pltpu.VMEM((NREP, 8, D), F32),
+            pltpu.VMEM((NREP, 1, D), F32),
             pltpu.VMEM((ZROWS, D), F32),
             pltpu.VMEM((CHIPS, CROWS, D), F32),
-            pltpu.VMEM((CHIPS, 8, D), F32),
+            pltpu.VMEM((CHIPS, 1, D), F32),
             pltpu.SemaphoreType.DMA((2, 64)),
             EXCHANGE_SEMS,
             EXCHANGE_SEMS,
@@ -594,13 +572,13 @@
             pltpu.VMEM((CL, KL + KH, TILE, TILE), BF16),
             pltpu.VMEM((D, D), BF16),
             pltpu.VMEM((2, D, D), F32),
-            pltpu.VMEM((8, D), F32),
+            pltpu.VMEM((1, D), F32),
             pltpu.VMEM((CL, TILE, D), F32),
             pltpu.VMEM((NEAR + 1, TILE, D), F32),
         ]
         + shift_scratch(room),
         compiler_params=pltpu.CompilerParams(
-            collective_id=room, has_side_effects=True, vmem_limit_bytes=VMEM_LIMIT
+            collective_id=2 + ROOMS.index(room), has_side_effects=True, vmem_limit_bytes=VMEM_LIMIT
         ),
     )(plan, order, back, tail, gp, gm, mean, home, moved, adjacency, w_self)
 
@@ -821,40 +799,42 @@
 FOUR = 4
 
 
-def final_kernel(first_ref, other_ref, more_ref, acc_ref, moved_ref, back_ref, passed_ref, *refs):
+def final_kernel(table_ref, acc_ref, moved_ref, back_ref, passed_ref, *refs):
     extra_ref = refs[0] if len(refs) == 8 else None
     dw_ref, db_ref, out_ref, dws_ref, dwn_ref, bias_ref, acc = refs[-7:]
     g = pl.program_id(0)
-    here_half = lax.rem(lax.axis_index("dom"), 2)
+    me = lax.axis_index("dom")
+    core, chip = lax.rem(me, 2), me // 2
     dws_ref[...] = dw_ref[0] * FACTOR
     dwn_ref[...] = dw_ref[1] * FACTOR
 
     @pl.when(g == 0)
     def _():
-        bias_ref[...] = jnp.sum(db_ref[...], axis=0, keepdims=True) * FACTOR
+        bias_ref[...] = db_ref[...] * FACTOR
         acc[...] = acc_ref[...]
         for j in range(MIG):
             acc[OWN + j] += moved_ref[j].astype(F32)
 
     for n in range(FOUR):
         c = g * FOUR + n
-        first, other = first_ref[c], other_ref[c]
+        first, asked = table_ref[c, me], table_ref[c, NDOM + chip]
+        other = lax.rem(asked, CL)
 
         @pl.when(first >= 0)
         def _():
             acc[first] += back_ref[n, pl.ds(0, TILE)].astype(F32)
 
-        @pl.when(other >= 0)
+        @pl.when(jnp.logical_and(asked >= 0, asked // CL == core))
         def _():
-            rows = pl.ds(pl.multiple_of(here_half * HALF, HALF), HALF)
+            rows = pl.ds(pl.multiple_of(core * HALF, HALF), HALF)
             acc[other, rows] += back_ref[n, pl.ds(TILE, HALF)].astype(F32)
-            rows = pl.ds(pl.multiple_of((1 - here_half) * HALF, HALF), HALF)
+            rows = pl.ds(pl.multiple_of((1 - core) * HALF, HALF), HALF)
             acc[other, rows] += passed_ref[n].astype(F32)
 
         if extra_ref is not None:
-            more = more_ref[c]
-
-            @pl.when(more >= 0)
+            more = table_ref[c, NDOM + CHIPS + chip]
+
+            @pl.when(jnp.logical_and(more >= 0, core == 1))
             def _():
                 acc[more] += extra_ref[n].astype(F32)
 
@@ -863,7 +843,7 @@
         out_ref[...] = acc[...].astype(BF16)
 
 
-def finish(first, other, more, acc, moved, back, passed, extra, dw, db):
+def finish(tables, acc, moved, back, passed, extra, dw, db):
     steps = NDOM // FOUR
 
     def four(rows):
@@ -879,18 +859,18 @@
             jax.ShapeDtypeStruct((1, D), F32),
         ],
         grid_spec=pltpu.PrefetchScalarGridSpec(
-            num_scalar_prefetch=3,
+            num_scalar_prefetch=1,
             grid=(steps,),
             in_specs=[whole(CL, TILE, D), whole(MIG, TILE, D), four(WIDE), four(HALF)]
             + [four(TILE)] * len(extras)
-            + [pl.BlockSpec((2, D // steps, D), lambda g, *_: (0, g, 0)), whole(8, D)],
+            + [pl.BlockSpec((2, D // steps, D), lambda g, *_: (0, g, 0)), whole(1, D)],
             out_specs=[whole(CL, TILE, D)]
             + [pl.BlockSpec((D // steps, D), lambda g, *_: (g, 0))] * 2
             + [whole(1, D)],
             scratch_shapes=[pltpu.VMEM((CL, TILE, D), F32)],
         ),
         compiler_params=pltpu.CompilerParams(vmem_limit_bytes=VMEM_LIMIT),
-    )(first, other, more, acc, moved, back, passed, *extras, dw, db)
+    )(tables, acc, moved, back, passed, *extras, dw, db)
 
 
 def requests(owner, local):
@@ -930,7 +910,7 @@
     adjacency, cotangent,
 ):
     me = lax.axis_index("dom")
-    core, chip = me % 2, me // 2
+    chip = me // 2
     home = features[0].reshape(CL, TILE, D)
     cot = cotangent[0].reshape(CL, TILE, D)
     src = local_source.reshape(-1)
@@ -940,22 +920,18 @@
     few = few_ways(offset)
     recv, tables, moved = lax.cond(
         few,
-        functools.partial(exchange_forward, 2),
-        functools.partial(exchange_forward, 3),
+        functools.partial(exchange_forward, ROOMS[0]),
+        functools.partial(exchange_forward, ROOMS[1]),
         cluster_plan,
         row.reshape(1, 128),
         home,
     )
     asked = tables[:, 0, :]
-    first = lax.dynamic_slice(asked, (0, me), (NDOM, 1)).reshape(-1)
-    other = lax.dynamic_slice(asked, (0, NDOM + chip), (NDOM, 1)).reshape(-1)
-    more = lax.dynamic_slice(asked, (0, NDOM + CHIPS + chip), (NDOM, 1)).reshape(-1)
-    other = jnp.where((other >= 0) & (other // CL == core), other % CL, -1)
-    more_here = jnp.where(core == 1, more, -1)
     order = sorted_near(src)
 
     def rest_of(extra, room, recv, moved):
         if extra:
+            more = lax.dynamic_slice(asked, (0, NDOM + CHIPS + chip), (NDOM, 1)).reshape(-1)
             recv = fourth_forward(more, home, recv)
         new, gp, mean, gm, tail, back = middle(
             blocks, src, recv.reshape(NDOM * UNITS, HALF, D), home, moved, adjacency, cot,
@@ -966,12 +942,12 @@
             room, cluster_plan, order, back, tail, gp, gm, mean, home, moved, adjacency, w_self
         )
         got = fourth_backward(back) if extra else None
-        return new, *finish(first, other, more_here, acc, returned, ret, passed, got, dw, db)
+        return new, *finish(asked, acc, returned, ret, passed, got, dw, db)
 
     extra = jnp.any(asked[:, NDOM + CHIPS : NDOM + 2 * CHIPS] >= 0)
     new, grad, dws, dwn, db = lax.switch(
         2 * extra.astype(jnp.int32) + 1 - few.astype(jnp.int32),
-        [functools.partial(rest_of, more, room) for more in (False, True) for room in (2, 3)],
+        [functools.partial(rest_of, more, room) for more in (False, True) for room in ROOMS],
         recv,
         moved,
     )

time: 366 us -> 267 us (0.73)
  the two profiles are of different devices: /device:TPU:1 before, /device:TPU:2 now
where the time goes in v1:
time: 267 us; the launch traced here: 262 us
  Pallas kernels  230 us (86%)
  loops' own time  16.5 us (6%)
  other arithmetic  6.54 us (2%)
  between operations  6.44 us (2%)
  local copies, waits for them, and re-layouts  2.9 us (1%)
    pallas_call x1, Pallas kernels, exchange_backward(): pl.pallas_call(functools.partial(backward_kernel, room), out_shape=[jax.S...  107 us
    pallas_call x1, Pallas kernels, exchange_forward(): pl.pallas_call(functools.partial(forward_kernel, room), out_shape=[jax.Sh...  95.6 us
    another operation x1, loops' own time, body(): lax.switch(2 * extra.astype(jnp.int32) + 1 - few.astype(jnp.int32), [func...  16.5 us
    pallas_call x1, Pallas kernels, middle(): pl.pallas_call(middle_kernel, out_shape=[tiles, tiles, tiles, tiles, jax....  15.2 us
    pallas_call x1, Pallas kernels, finish(): pl.pallas_call(final_kernel, out_shape=[jax.ShapeDtypeStruct((CL, TILE, D...  11.6 us

profile of v1, /device:TPU:2, one launch (start us, length us, event | category | flops | bytes accessed | tf_op | source)
XLA Modules:
  0.0 262.3 jit_solution(12696668081752953322)
XLA Ops:
  0.6 0.7 broadcast_subtract_fusion
  1.6 0.1 fusion.13
  1.7 0.6 compare_reduce_fusion.5
  2.3 0.6 compare_reduce_fusion.3
  4.9 0.6 compare_reduce_fusion.2
  6.2 0.6 compare_reduce_fusion
  8.1 0.8 copy.27
  9.0 0.2 fusion.9
  9.2 0.2 and_reduce_fusion
  9.4 0.8 copy.28
  10.3 97.0 %conditional.2 = (s32[32,128]{1,0:T(8,128)}, (bf16[32,320,512]{2,1,0:T(8,128)(2,1)}, s32[32,1,128]{2,1,0:T(1,128)S(1)}, bf16[3,128,512]{2,1,0:T(8,128)(2,1)S(1)})) conditional(s32[]{:T(128)} %convert_element_type.35, (s32[16]{0:T(128)}, pred[32]{0:T(512)(128)(4,1)S(1)}, bf16[16,128,512]{2,1,0:T(8,128)(2,1)}, s32[]{:T(128)}, ...), branch_computations={%region_15.16_spmd.clone.clone, %region_16.17_spmd.clone.clone} | conditional | flops 12608 | bytes 52152 | solution.py:921
  10.3 0.1 select_reduce_fusion.1
  10.4 0.5 add_bitcast_fusion.1.row_ref
  11.0 95.6 %branch_1_fun.8 = (bf16[32,320,512]{2,1,0:T(8,128)(2,1)}, s32[32,1,128]{2,1,0:T(1,128)}, bf16[3,128,512]{2,1,0:T(8,128)(2,1)S(1)}) custom-call(s32[16]{0:T(128)} %get-tuple-element.605.plan_ref, s32[1,128]{1,0:T(1,128)} %add_bitcast_fusion.1.row_ref, bf16[16,128,512]{2,1,0:T(8,128)(2,1)} %get-tuple-element.606.home_ref), custom_call_target="tpu_custom_call" | custom-call | tf_op jit(solution)/shard_map/cond/branch_1_fun/pallas_call | solution.py:327
  106.6 0.7 copy.65
  107.3 1.4 fusion.10
  109.6 0.1 reshape.402
  109.9 0.1 convert_reduce_fusion.1
  110.0 0.2 convert_reduce_fusion
  110.2 0.1 select_reduce_fusion.2
  110.4 150.8 %conditional.3 = (bf16[16,128,512]{2,1,0:T(8,128)(2,1)}, bf16[16,128,512]{2,1,0:T(8,128)(2,1)}, f32[512,512]{1,0:T(8,128)}, f32[512,512]{1,0:T(8,128)}, f32[1,512]{1,0:T(1,128)}) conditional(s32[]{:T(128)} %clamp.3, (bf16[32,320,512]{2,1,0:T(8,128)(2,1)}, s32[64]{0:T(128)S(1)}, s32[48]{0:T(128)S(1)}, ...), branch_computations={%region_21.22_spmd, %region_22.23_spmd, %region_23.24_spmd, %regio... | conditional | flops 19 | bytes 8389416 | solution.py:948
  110.8 15.2 %branch_0_fun.5 = (bf16[16,128,512]{2,1,0:T(8,128)(2,1)}, bf16[16,128,512]{2,1,0:T(8,128)(2,1)}, bf16[16,128,512]{2,1,0:T(8,128)(2,1)}, bf16[16,128,512]{2,1,0:T...) custom-call(s32[64]{0:T(128)S(1)} %get-tuple-element.273.block_ref, ...), custom_call_target="tpu_custom_call" | custom-call | tf_op jit(solution)/shard_map/cond/branch_0_fun/pallas_call | solution.py:765
  126.0 107.4 %branch_0_fun.6 = (bf16[32,192,512]{2,1,0:T(8,128)(2,1)}, bf16[32,64,512]{2,1,0:T(8,128)(2,1)}, bf16[3,128,512]{2,1,0:T(8,128)(2,1)}, f32[16,128,512]{2,1,0:T(8,...) custom-call(s32[16]{0:T(128)S(1)} %copy-done.7, s32[65]{0:T(128)S(1)} %get-tuple-element.286.order_ref, ...), custom_call_target="tpu_custom_call" | custom-call | tf_op jit(solution)/shard_map/cond/branch_0_fun/pallas_call | solution.py:542
  233.4 11.6 %branch_0_fun.7 = (bf16[16,128,512]{2,1,0:T(8,128)(2,1)}, f32[512,512]{1,0:T(8,128)}, f32[512,512]{1,0:T(8,128)}, f32[1,512]{1,0:T(1,128)}) custom-call(s32[32,128]{1,0:T(8,128)} %get-tuple-element.284.table_ref, f32[16,128,512]{2,1,0:T(8,128)} %get-tuple-element.292.acc_ref, bf16[3,128,512]{2,1,0:T(8,128)(2,1)} %get-tuple-element.293.moved_ref, ...), custom_call_target="tpu_custom_call" | custom-call | tf_op jit(solution)/shard_map/cond/branch_0_fun/pallas_call | solution.py:853
  (30 shorter events, 0.9 us)
Async XLA Ops:
  10.3 99.5 %copy-start.11 = (s32[16,3]{0,1:T(4,128)S(1)}, s32[16,3]{0,1:T(4,128)}, u32[]{:S(2)}) copy-start(s32[16,3]{0,1:T(4,128)} %param.21) | copy-start | bytes 580
  10.3 100.1 %copy-start.4 = (bf16[512,512]{1,0:T(8,128)(2,1)S(1)}, bf16[512,512]{1,0:T(8,128)(2,1)}, u32[]{:S(2)}) copy-start(bf16[512,512]{1,0:T(8,128)(2,1)} %param.17) | copy-start | bytes 1572868
  10.3 100.1 %copy-start.5 = (bf16[512,512]{1,0:T(8,128)(2,1)S(1)}, bf16[512,512]{1,0:T(8,128)(2,1)}, u32[]{:S(2)}) copy-start(bf16[512,512]{1,0:T(8,128)(2,1)} %param.18) | copy-start | bytes 1572868
  10.3 100.1 %copy-start.6 = (f32[512]{0:T(512)S(1)}, f32[512]{0:T(512)}, u32[]{:S(2)}) copy-start(f32[512]{0:T(512)} %param.19) | copy-start | bytes 6148
  110.8 15.2 %copy-start = (bf16[16,128,512]{2,1,0:T(8,128)(2,1)S(1)}, bf16[16,128,512]{2,1,0:T(8,128)(2,1)}, u32[]{:S(2)}) copy-start(bf16[16,128,512]{2,1,0:T(8,128)(2,1)} %get-tuple-element.276.refs_16_.home_ref) | copy-start | bytes 6291460 | tf_op jit(solution)/shard_map/cond
  110.8 15.2 %copy-start.7 = (s32[16]{0:T(128)S(1)}, s32[16]{0:T(128)}, u32[]{:S(2)}) copy-start(s32[16]{0:T(128)} %get-tuple-element.285.plan_ref) | copy-start | bytes 196 | tf_op jit(solution)/shard_map/cond

commit v2 on v1

--- a/solution.py
+++ b/solution.py
@@ -253,13 +253,13 @@
     shift = (signed >> 1) + ((core + swap) & 1) * swap
     along_x = shift & (SIDE - 1)
     along_y = ((shift >> 2) + ((x + along_x) >> 2)) & (SIDE - 1)
-    fits = jnp.bool_(True)
-    for steps in (jnp.broadcast_to(along_x, along_y.shape), along_y):
-        steps = jnp.where(back == 1, (SIDE - steps) & (SIDE - 1), steps)
-        for way, step in enumerate((1, SIDE - 1, 2)):
-            count = jnp.sum((steps == step).astype(jnp.int32), axis=-1)
-            fits = fits & jnp.all(count <= ROOMS[0][way])
-    return fits
+    axes = jnp.stack([jnp.broadcast_to(along_x, along_y.shape), along_y])
+    axes = jnp.where(back == 1, (SIDE - axes) & (SIDE - 1), axes)
+    crowded = jnp.zeros(axes.shape[:-1], jnp.bool_)
+    for way, step in enumerate((1, SIDE - 1, 2)):
+        count = sum((axes[..., j] == step).astype(jnp.int32) for j in range(MIG))
+        crowded = crowded | (count > ROOMS[0][way])
+    return ~jnp.any(crowded)
 
 
 EXCHANGE_SEMS = pltpu.SemaphoreType.DMA((2, NPEER))
@@ -312,11 +312,11 @@
     )
     keep.start()
     tiles = Exchange(here, stage, recv_ref, tile_sems.at[0], tile_sems.at[1], 0, WIDE)
-    tiles.start(0, 3)
+    tiles.start(0, 4)
     shift.turn()
-    tiles.start(3, 7)
+    tiles.start(4, 8)
     shift.start_lane()
-    tiles.start(7, WIDE // CHUNK)
+    tiles.start(8, WIDE // CHUNK)
     keep.wait()
     for n in range(NPEER):
         tiles.every(n).wait()
@@ -685,83 +685,112 @@
     )(back)
 
 
-def tile_block(width=D):
-    return pl.BlockSpec((GROUP, TILE, width), lambda g, *_: (g, 0, 0))
-
-
-def whole(*shape):
-    return pl.BlockSpec(shape, lambda g, *_: (0,) * len(shape))
-
-
-def adj_block(k):
-    return pl.BlockSpec((GROUP, 1, TILE, TILE), lambda g, *_: (g, k, 0, 0))
-
-
-def own_tile(i, g, home_tile, moved_ref):
-    j = CL - GROUP + i - OWN
-    if j < 0:
-        return home_tile
-    return jnp.where(g == STEPS - 1, moved_ref[j], home_tile)
-
-
-PARTS = 2 * GROUP * KH
-
-
-def middle_kernel(block_ref, src_ref, *refs):
-    halo = refs[:PARTS]
-    (home_ref, moved_ref, adj_ref, cot_ref, ws_ref, wn_ref, bias_ref) = refs[PARTS : PARTS + 7]
-    (new_ref, gp_ref, mean_ref, gm_ref, tail_ref, back_ref) = refs[PARTS + 7 : PARTS + 13]
-    (own, scale, grads, sem) = refs[PARTS + 13 :]
-    g = pl.program_id(0)
-    for i in range(GROUP):
-        slot = g * GROUP + i
-        rows = pl.ds(i * TILE, TILE)
-        mine = own_tile(i, g, home_ref[slot], moved_ref)
-        own[rows] = mine
-        adj = jnp.concatenate([adj_ref[i, k] for k in range(KL + KH)], axis=1)
-        total = jnp.sum(adj.astype(F32), axis=1, keepdims=True)
-        scale[rows] = jnp.broadcast_to(1.0 / (1.0 + total), (TILE, D))
-        near = [home_ref[src_ref[slot * KL + k]] for k in range(KL)]
-        far = [halo[2 * KH * i + n][0] for n in range(2 * KH)]
-        agg = mine.astype(F32) + dot_nn(adj, jnp.concatenate(near + far, axis=0))
-        mean_ref[i] = (agg * scale[rows]).astype(BF16)
-    pre = (
-        dot_nn(own[...], ws_ref[...])
-        + dot_nn(mean_ref[...].reshape(ROWS, D), wn_ref[...])
-        + bias_ref[...]
-    )
-    sig = 1.0 / (1.0 + jnp.exp(-pre))
-    new_ref[...] = (pre * sig).astype(BF16).reshape(GROUP, TILE, D)
-    cot = cot_ref[...].reshape(ROWS, D).astype(F32)
-    gp = (cot * sig * (1.0 + pre * (1.0 - sig))).astype(BF16)
-    gp_ref[...] = gp.reshape(GROUP, TILE, D)
-    gm = (dot_nt(gp, wn_ref[...]) * scale[...]).astype(BF16)
-    gm_ref[...] = gm.reshape(GROUP, TILE, D)
-
-    def copy(n):
-        return pltpu.make_async_copy(grads.at[n], back_ref.at[block_ref[n]], sem.at[n])
-
-    for i in range(GROUP):
-        adj = jnp.concatenate([adj_ref[i, KL + k] for k in range(KH)], axis=1)
-        both = dot_tn(adj, gm[i * TILE : (i + 1) * TILE]).astype(BF16)
-        for part in range(2 * KH):
-            n = (g * GROUP + i) * 2 * KH + part
-            grads[n] = both[part * HALF : (part + 1) * HALF]
-            copy(n).start()
-
-    @pl.when(g == STEPS - 1)
-    def _():
-        first = TILE * (GROUP - MIG)
-        tail = dot_nt(gp[first:], ws_ref[...]) + gm[first:].astype(F32)
-        tail_ref[...] = tail.astype(BF16).reshape(MIG, TILE, D)
-        loop(0, 2 * CL * KH, lambda n: copy(n).wait())
+def middle_kernel(
+    block_ref, src_ref, recv_ref, home_ref, moved_ref, adj_ref, cot_ref, ws_ref, wn_ref, bias_ref,
+    new_ref, gp_ref, mean_ref, gm_ref, tail_ref, back_ref,
+    halo, home, adj, cot, ws, wn, own, scale, new, gp, mean, gm, grads, halo_sem, in_sem, out_sem, back_sem,
+):
+    parts = 2 * KH * GROUP
+
+    def copy_halo(n):
+        return pltpu.make_async_copy(recv_ref.at[block_ref[n]], halo.at[n], halo_sem.at[n])
+
+    def copy_back(n):
+        return pltpu.make_async_copy(grads.at[n], back_ref.at[block_ref[n]], back_sem.at[n])
+
+    def group(g):
+        return pl.ds(g * GROUP, GROUP)
+
+    def copy_in(g, ref, held, n):
+        return pltpu.make_async_copy(ref.at[group(g)], held.at[group(g)], in_sem.at[n, g])
+
+    def copy_out(g, n):
+        held, ref = ((new, new_ref), (gp, gp_ref), (mean, mean_ref), (gm, gm_ref))[n]
+        return pltpu.make_async_copy(held.at[group(g)], ref.at[group(g)], out_sem.at[n, g])
+
+    once = [
+        pltpu.make_async_copy(ref, held, in_sem.at[2, n])
+        for n, (ref, held) in enumerate([(home_ref, home), (ws_ref, ws), (wn_ref, wn)])
+    ]
+    once[0].start()
+
+    def start(g):
+        copy_in(g, adj_ref, adj, 0).start()
+        loop(0, parts, lambda n: copy_halo(g * parts + n).start())
+        copy_in(g, cot_ref, cot, 1).start()
+
+    start(0)
+    once[1].start()
+    once[2].start()
+    loop(1, STEPS, start)
+    once[0].wait()
+
+    def step(g):
+        copy_in(g, adj_ref, adj, 0).wait()
+        loop(0, parts, lambda n: copy_halo(g * parts + n).wait())
+        for i in range(GROUP):
+            slot = g * GROUP + i
+            rows = pl.ds(i * TILE, TILE)
+            mine = home[slot]
+            if STEPS * GROUP - GROUP + i >= OWN:
+                mine = jnp.where(g == STEPS - 1, moved_ref[CL - GROUP + i - OWN], mine)
+            own[rows] = mine
+            tiles = jnp.concatenate([adj[slot, k] for k in range(KL + KH)], axis=1)
+            total = jnp.sum(tiles.astype(F32), axis=1, keepdims=True)
+            scale[rows] = jnp.broadcast_to(1.0 / (1.0 + total), (TILE, D))
+            near = [home[src_ref[slot * KL + k]] for k in range(KL)]
+            far = halo[pl.ds(slot * 2 * KH, 2 * KH)].reshape(KH * TILE, D)
+            agg = mine.astype(F32) + dot_nn(tiles, jnp.concatenate(near + [far], axis=0))
+            mean[slot] = (agg * scale[rows]).astype(BF16)
+        copy_out(g, 2).start()
+
+        @pl.when(g == 0)
+        def _():
+            once[1].wait()
+            once[2].wait()
+
+        pre = (
+            dot_nn(own[...], ws[...])
+            + dot_nn(mean[group(g)].reshape(ROWS, D), wn[...])
+            + bias_ref[...]
+        )
+        sig = 1.0 / (1.0 + jnp.exp(-pre))
+        new[group(g)] = (pre * sig).astype(BF16).reshape(GROUP, TILE, D)
+        copy_out(g, 0).start()
+        copy_in(g, cot_ref, cot, 1).wait()
+        grad_out = cot[group(g)].reshape(ROWS, D).astype(F32)
+        grad = (grad_out * sig * (1.0 + pre * (1.0 - sig))).astype(BF16)
+        gp[group(g)] = grad.reshape(GROUP, TILE, D)
+        copy_out(g, 1).start()
+        grad_mean = (dot_nt(grad, wn[...]) * scale[...]).astype(BF16)
+        gm[group(g)] = grad_mean.reshape(GROUP, TILE, D)
+        copy_out(g, 3).start()
+        for i in range(GROUP):
+            slot = g * GROUP + i
+            tiles = jnp.concatenate([adj[slot, KL + k] for k in range(KH)], axis=1)
+            both = dot_tn(tiles, grad_mean[i * TILE : (i + 1) * TILE]).astype(BF16)
+            grads[pl.ds(slot * 2 * KH, 2 * KH)] = both.reshape(2 * KH, HALF, D)
+            for part in range(2 * KH):
+                copy_back(slot * 2 * KH + part).start()
+
+    loop(0, STEPS, step)
+    first = pl.ds(OWN, MIG)
+    tail = dot_nt(gp[first].reshape(MIG * TILE, D), ws[...])
+    tail = tail + gm[first].reshape(MIG * TILE, D).astype(F32)
+    tail_ref[...] = tail.astype(BF16).reshape(MIG, TILE, D)
+
+    def finish(g):
+        for n in range(4):
+            copy_out(g, n).wait()
+        loop(0, parts, lambda n: copy_back(g * parts + n).wait())
+
+    loop(0, STEPS, finish)
 
 
 def middle(blocks, src, recv, home, moved, adjacency, cot, w_self, w_neigh, bias):
-    def halo_block(n):
-        return pl.BlockSpec((1, HALF, D), lambda g, blocks, src: (blocks[g * PARTS + n], 0, 0))
-
     tiles = jax.ShapeDtypeStruct((CL, TILE, D), BF16)
+    held = pltpu.VMEM((CL, TILE, D), BF16)
+    pieces = pltpu.VMEM((2 * CL * KH, HALF, D), BF16)
     return pl.pallas_call(
         middle_kernel,
         out_shape=[
@@ -771,84 +800,122 @@
         ],
         grid_spec=pltpu.PrefetchScalarGridSpec(
             num_scalar_prefetch=2,
-            grid=(STEPS,),
-            in_specs=[halo_block(n) for n in range(PARTS)]
-            + [
-                whole(CL, TILE, D),
-                whole(MIG, TILE, D),
-                pl.BlockSpec((GROUP, KL + KH, TILE, TILE), lambda g, *_: (g, 0, 0, 0)),
-                tile_block(),
-                whole(D, D),
-                whole(D, D),
-                whole(1, D),
-            ],
-            out_specs=[tile_block()] * 4 + [whole(MIG, TILE, D), ANY],
+            grid=(),
+            in_specs=[ANY, ANY, VMEM, ANY, ANY, ANY, ANY, VMEM],
+            out_specs=[ANY] * 4 + [VMEM, ANY],
             scratch_shapes=[
+                pieces,
+                held,
+                pltpu.VMEM((CL, KL + KH, TILE, TILE), BF16),
+                held,
+                pltpu.VMEM((D, D), BF16),
+                pltpu.VMEM((D, D), BF16),
                 pltpu.VMEM((ROWS, D), BF16),
                 pltpu.VMEM((ROWS, D), F32),
-                pltpu.VMEM((2 * CL * KH, HALF, D), BF16),
+                held,
+                held,
+                held,
+                held,
+                pieces,
+                pltpu.SemaphoreType.DMA((2 * CL * KH,)),
+                pltpu.SemaphoreType.DMA((3, STEPS)),
+                pltpu.SemaphoreType.DMA((4, STEPS)),
                 pltpu.SemaphoreType.DMA((2 * CL * KH,)),
             ],
         ),
         compiler_params=pltpu.CompilerParams(vmem_limit_bytes=VMEM_LIMIT),
-    )(
-        blocks, src, *([recv] * PARTS), home, moved, adjacency, cot, w_self, w_neigh, bias
-    )
+    )(blocks, src, recv, home, moved, adjacency, cot, w_self, w_neigh, bias)
 
 
 FOUR = 4
 
 
-def final_kernel(table_ref, acc_ref, moved_ref, back_ref, passed_ref, *refs):
-    extra_ref = refs[0] if len(refs) == 8 else None
-    dw_ref, db_ref, out_ref, dws_ref, dwn_ref, bias_ref, acc = refs[-7:]
-    g = pl.program_id(0)
+def final_kernel(table_ref, acc_ref, moved_ref, db_ref, dw_ref, back_ref, passed_ref, *refs):
+    extra_ref, more = (refs[0], refs[-1]) if len(refs) == 14 else (None, None)
+    refs = refs if extra_ref is None else refs[1:]
+    out_ref, dws_ref, dwn_ref, bias_ref = refs[:4]
+    acc, out, dw, back, passed, in_sem, chunk_sem, out_sem = refs[4:12]
     me = lax.axis_index("dom")
     core, chip = lax.rem(me, 2), me // 2
-    dws_ref[...] = dw_ref[0] * FACTOR
-    dwn_ref[...] = dw_ref[1] * FACTOR
-
-    @pl.when(g == 0)
-    def _():
-        bias_ref[...] = db_ref[...] * FACTOR
-        acc[...] = acc_ref[...]
-        for j in range(MIG):
-            acc[OWN + j] += moved_ref[j].astype(F32)
-
-    for n in range(FOUR):
-        c = g * FOUR + n
-        first, asked = table_ref[c, me], table_ref[c, NDOM + chip]
-        other = lax.rem(asked, CL)
-
-        @pl.when(first >= 0)
-        def _():
-            acc[first] += back_ref[n, pl.ds(0, TILE)].astype(F32)
-
-        @pl.when(jnp.logical_and(asked >= 0, asked // CL == core))
-        def _():
-            rows = pl.ds(pl.multiple_of(core * HALF, HALF), HALF)
-            acc[other, rows] += back_ref[n, pl.ds(TILE, HALF)].astype(F32)
-            rows = pl.ds(pl.multiple_of((1 - core) * HALF, HALF), HALF)
-            acc[other, rows] += passed_ref[n].astype(F32)
-
-        if extra_ref is not None:
-            more = table_ref[c, NDOM + CHIPS + chip]
-
-            @pl.when(jnp.logical_and(more >= 0, core == 1))
+    steps = NDOM // FOUR
+    pairs = [(back_ref, back), (passed_ref, passed)]
+    if extra_ref is not None:
+        pairs.append((extra_ref, more))
+
+    def chunk(q, n):
+        ref, held = pairs[n]
+        some = pl.ds(q * FOUR, FOUR)
+        return pltpu.make_async_copy(ref.at[some], held.at[some], chunk_sem.at[n, q])
+
+    take_acc = pltpu.make_async_copy(acc_ref, acc, in_sem.at[0])
+    take_dw = pltpu.make_async_copy(dw_ref, dw, in_sem.at[1])
+    take_acc.start()
+
+    def start(q):
+        for n in range(len(pairs)):
+            chunk(q, n).start()
+
+    loop(0, 1, start)
+    take_dw.start()
+    loop(1, steps, start)
+    bias_ref[...] = db_ref[...] * FACTOR
+    take_acc.wait()
+    for j in range(MIG):
+        acc[OWN + j] += moved_ref[j].astype(F32)
+
+    def add(q):
+        for n in range(len(pairs)):
+            chunk(q, n).wait()
+        for n in range(FOUR):
+            c = q * FOUR + n
+            first, asked = table_ref[c, me], table_ref[c, NDOM + chip]
+            other = lax.rem(asked, CL)
+
+            @pl.when(first >= 0)
             def _():
-                acc[more] += extra_ref[n].astype(F32)
-
-    @pl.when(g == NDOM // FOUR - 1)
-    def _():
-        out_ref[...] = acc[...].astype(BF16)
+                acc[first] += back[c, pl.ds(0, TILE)].astype(F32)
+
+            @pl.when(jnp.logical_and(asked >= 0, asked // CL == core))
+            def _():
+                rows = pl.ds(pl.multiple_of(core * HALF, HALF), HALF)
+                acc[other, rows] += back[c, pl.ds(TILE, HALF)].astype(F32)
+                rows = pl.ds(pl.multiple_of((1 - core) * HALF, HALF), HALF)
+                acc[other, rows] += passed[c].astype(F32)
+
+            if extra_ref is not None:
+                fourth = table_ref[c, NDOM + CHIPS + chip]
+
+                @pl.when(jnp.logical_and(fourth >= 0, core == 1))
+                def _():
+                    acc[fourth] += more[c].astype(F32)
+
+    loop(0, steps // 2, add)
+    take_dw.wait()
+    give = [
+        pltpu.make_async_copy(dw.at[n], ref, out_sem.at[n])
+        for n, ref in enumerate((dws_ref, dwn_ref))
+    ]
+    for n in range(2):
+        dw[n] = dw[n] * FACTOR
+        give[n].start()
+    loop(steps // 2, steps, add)
+
+    def give_out(g):
+        some = pl.ds(g * GROUP, GROUP)
+        return pltpu.make_async_copy(out.at[some], out_ref.at[some], out_sem.at[2 + g])
+
+    def settle(g):
+        some = pl.ds(g * GROUP, GROUP)
+        out[some] = acc[some].astype(BF16)
+        give_out(g).start()
+
+    loop(0, STEPS, settle)
+    for copy in give:
+        copy.wait()
+    loop(0, STEPS, lambda g: give_out(g).wait())
 
 
 def finish(tables, acc, moved, back, passed, extra, dw, db):
-    steps = NDOM // FOUR
-
-    def four(rows):
-        return pl.BlockSpec((FOUR, rows, D), lambda g, *_: (g, 0, 0))
-
     extras = [] if extra is None else [extra]
     return pl.pallas_call(
         final_kernel,
@@ -860,17 +927,23 @@
         ],
         grid_spec=pltpu.PrefetchScalarGridSpec(
             num_scalar_prefetch=1,
-            grid=(steps,),
-            in_specs=[whole(CL, TILE, D), whole(MIG, TILE, D), four(WIDE), four(HALF)]
-            + [four(TILE)] * len(extras)
-            + [pl.BlockSpec((2, D // steps, D), lambda g, *_: (0, g, 0)), whole(1, D)],
-            out_specs=[whole(CL, TILE, D)]
-            + [pl.BlockSpec((D // steps, D), lambda g, *_: (g, 0))] * 2
-            + [whole(1, D)],
-            scratch_shapes=[pltpu.VMEM((CL, TILE, D), F32)],
+            grid=(),
+            in_specs=[ANY, VMEM, VMEM, ANY, ANY, ANY] + [ANY] * len(extras),
+            out_specs=[ANY, ANY, ANY, VMEM],
+            scratch_shapes=[
+                pltpu.VMEM((CL, TILE, D), F32),
+                pltpu.VMEM((CL, TILE, D), BF16),
+                pltpu.VMEM((2, D, D), F32),
+                pltpu.VMEM((NDOM, WIDE, D), BF16),
+                pltpu.VMEM((NDOM, HALF, D), BF16),
+                pltpu.SemaphoreType.DMA((2,)),
+                pltpu.SemaphoreType.DMA((3, NDOM // FOUR)),
+                pltpu.SemaphoreType.DMA((2 + STEPS,)),
+            ]
+            + [pltpu.VMEM((NDOM, TILE, D), BF16)] * len(extras),
         ),
         compiler_params=pltpu.CompilerParams(vmem_limit_bytes=VMEM_LIMIT),
-    )(tables, acc, moved, back, passed, *extras, dw, db)
+    )(tables, acc, moved, db, dw, back, passed, *extras)
 
 
 def requests(owner, local):

time: 267 us -> 258 us (0.966)
  the two profiles are of different devices: /device:TPU:2 before, /device:TPU:3 now
where the time goes in v2:
time: 258 us; the launch traced here: 254 us
  Pallas kernels  227 us (88%)
  loops' own time  16.6 us (6%)
  other arithmetic  4.68 us (2%)
  between operations  3.18 us (1%)
  local copies, waits for them, and re-layouts  2.97 us (1%)
    pallas_call x1, Pallas kernels, exchange_backward(): pl.pallas_call(functools.partial(backward_kernel, room), out_shape=[jax.S...  107 us
    pallas_call x1, Pallas kernels, exchange_forward(): pl.pallas_call(functools.partial(forward_kernel, room), out_shape=[jax.Sh...  95 us
    another operation x1, loops' own time, body(): lax.switch(2 * extra.astype(jnp.int32) + 1 - few.astype(jnp.int32), [func...  16.6 us
    pallas_call x1, Pallas kernels, middle(): pl.pallas_call(middle_kernel, out_shape=[tiles, tiles, tiles, tiles, jax....  15.1 us
    pallas_call x1, Pallas kernels, finish(): pl.pallas_call(final_kernel, out_shape=[jax.ShapeDtypeStruct((CL, TILE, D...  9.59 us

profile of v2, /device:TPU:3, one launch (start us, length us, event | category | flops | bytes accessed | tf_op | source)
XLA Modules:
  0.0 254.2 jit_solution(13155273915668619260)
XLA Ops:
  0.6 0.7 broadcast_subtract_fusion
  1.8 0.7 or_reduce_fusion
  3.1 0.8 copy.27
  3.9 0.1 eq.144
  3.9 0.2 fusion.9
  4.2 0.2 and_reduce_fusion
  4.4 0.8 copy.28
  5.1 0.1 reshape.460
  5.3 96.4 %conditional.2 = (s32[32,128]{1,0:T(8,128)}, (bf16[32,320,512]{2,1,0:T(8,128)(2,1)}, s32[32,1,128]{2,1,0:T(1,128)S(1)}, bf16[3,128,512]{2,1,0:T(8,128)(2,1)S(1)})) conditional(s32[]{:T(128)} %convert_element_type.56, (s32[16]{0:T(128)}, pred[32]{0:T(512)(128)(4,1)S(1)}, bf16[16,128,512]{2,1,0:T(8,128)(2,1)}, s32[]{:T(128)}, ...), branch_computations={%region_4.5_spmd.clone.clone, %region_5.6_spmd.clone.clone} | conditional | flops 12608 | bytes 52152 | solution.py:994
  5.3 0.1 select_reduce_fusion.1
  5.4 0.5 add_bitcast_fusion.1.row_ref
  5.9 95.0 %branch_1_fun.8 = (bf16[32,320,512]{2,1,0:T(8,128)(2,1)}, s32[32,1,128]{2,1,0:T(1,128)}, bf16[3,128,512]{2,1,0:T(8,128)(2,1)S(1)}) custom-call(s32[16]{0:T(128)} %get-tuple-element.605.plan_ref, s32[1,128]{1,0:T(1,128)} %add_bitcast_fusion.1.row_ref, bf16[16,128,512]{2,1,0:T(8,128)(2,1)} %get-tuple-element.606.home_ref), custom_call_target="tpu_custom_call" | custom-call | tf_op jit(solution)/shard_map/cond/branch_1_fun/pallas_call | solution.py:327
  100.9 0.7 copy.65
  101.6 1.4 fusion.10
  103.9 0.1 copy.30
  103.9 0.1 reshape.462
  104.1 0.1 reshape.463
  104.2 0.1 convert_reduce_fusion.1
  104.4 0.2 convert_reduce_fusion
  104.5 0.1 select_reduce_fusion.2
  104.7 148.3 %conditional.3 = (bf16[16,128,512]{2,1,0:T(8,128)(2,1)}, bf16[16,128,512]{2,1,0:T(8,128)(2,1)}, f32[512,512]{1,0:T(8,128)}, f32[512,512]{1,0:T(8,128)}, f32[1,512]{1,0:T(1,128)}) conditional(s32[]{:T(128)} %clamp.3, (bf16[32,320,512]{2,1,0:T(8,128)(2,1)}, s32[64]{0:T(128)S(1)}, s32[48]{0:T(128)S(1)}, ...), branch_computations={%region_10.11_spmd, %region_11.12_spmd, %region_12.13_spmd, %regio... | conditional | flops 19 | bytes 8389416 | solution.py:1021
  105.1 15.1 %branch_0_fun.5 = (bf16[16,128,512]{2,1,0:T(8,128)(2,1)}, bf16[16,128,512]{2,1,0:T(8,128)(2,1)}, bf16[16,128,512]{2,1,0:T(8,128)(2,1)}, bf16[16,128,512]{2,1,0:T...) custom-call(s32[64]{0:T(128)S(1)} %get-tuple-element.273.block_ref, ...), custom_call_target="tpu_custom_call" | custom-call | tf_op jit(solution)/shard_map/cond/branch_0_fun/pallas_call | solution.py:794
  120.3 107.0 %branch_0_fun.6 = (bf16[32,192,512]{2,1,0:T(8,128)(2,1)}, bf16[32,64,512]{2,1,0:T(8,128)(2,1)}, bf16[3,128,512]{2,1,0:T(8,128)(2,1)}, f32[16,128,512]{2,1,0:T(8,...) custom-call(s32[16]{0:T(128)S(1)} %copy-done.7, s32[65]{0:T(128)S(1)} %get-tuple-element.286.order_ref, ...), custom_call_target="tpu_custom_call" | custom-call | tf_op jit(solution)/shard_map/cond/branch_0_fun/pallas_call | solution.py:542
  227.3 9.6 %branch_0_fun.7 = (bf16[16,128,512]{2,1,0:T(8,128)(2,1)}, f32[512,512]{1,0:T(8,128)}, f32[512,512]{1,0:T(8,128)}, f32[1,512]{1,0:T(1,128)}) custom-call(s32[32,128]{1,0:T(8,128)} %get-tuple-element.284.table_ref, f32[16,128,512]{2,1,0:T(8,128)} %get-tuple-element.292.acc_ref, bf16[3,128,512]{2,1,0:T(8,128)(2,1)} %get-tuple-element.293.moved_ref, ...), custom_call_target="tpu_custom_call" | custom-call | tf_op jit(solution)/shard_map/cond/branch_0_fun/pallas_call | solution.py:920
  (28 shorter events, 0.7 us)
Async XLA Ops:
  5.2 98.8 %copy-start.11 = (s32[16,3]{0,1:T(4,128)S(1)}, s32[16,3]{0,1:T(4,128)}, u32[]{:S(2)}) copy-start(s32[16,3]{0,1:T(4,128)} %param.21) | copy-start | bytes 580
  5.2 99.5 %copy-start.4 = (bf16[512,512]{1,0:T(8,128)(2,1)S(1)}, bf16[512,512]{1,0:T(8,128)(2,1)}, u32[]{:S(2)}) copy-start(bf16[512,512]{1,0:T(8,128)(2,1)} %param.17) | copy-start | bytes 1572868
  5.2 99.5 %copy-start.5 = (bf16[512,512]{1,0:T(8,128)(2,1)S(1)}, bf16[512,512]{1,0:T(8,128)(2,1)}, u32[]{:S(2)}) copy-start(bf16[512,512]{1,0:T(8,128)(2,1)} %param.18) | copy-start | bytes 1572868
  5.2 99.5 %copy-start.6 = (f32[512]{0:T(512)S(1)}, f32[512]{0:T(512)}, u32[]{:S(2)}) copy-start(f32[512]{0:T(512)} %param.19) | copy-start | bytes 6148
  105.1 15.2 %copy-start = (bf16[16,128,512]{2,1,0:T(8,128)(2,1)S(1)}, bf16[16,128,512]{2,1,0:T(8,128)(2,1)}, u32[]{:S(2)}) copy-start(bf16[16,128,512]{2,1,0:T(8,128)(2,1)} %get-tuple-element.276.home_ref) | copy-start | bytes 6291460 | tf_op jit(solution)/shard_map/cond
  105.1 15.2 %copy-start.7 = (s32[16]{0:T(128)S(1)}, s32[16]{0:T(128)}, u32[]{:S(2)}) copy-start(s32[16]{0:T(128)} %get-tuple-element.285.plan_ref) | copy-start | bytes 196 | tf_op jit(solution)/shard_map/cond

commit v3 on v2

--- a/solution.py
+++ b/solution.py
@@ -203,8 +203,8 @@
             along_x.append(lax.rem(shift, SIDE))
             along_y.append(lax.rem(shift // SIDE + carry, SIDE))
             self.swaps.append(swap)
-        self.x = Ring(here, along_x, "x", sign, room, ring_x, self.sems.at[0])
-        self.y = Ring(here, along_y, "y", sign, room, ring_y, self.sems.at[1])
+        self.x = Ring(here, along_x, "x", sign, room[0], ring_x, self.sems.at[0])
+        self.y = Ring(here, along_y, "y", sign, room[1], ring_y, self.sems.at[1])
 
     def copy_lane(self):
         slot = self.lanes.at[self.here.core]
@@ -229,16 +229,18 @@
             out_ref[j] = self.lanes[lax.rem(self.here.core + self.swaps[j], 2), j]
 
 
-ROOMS = [(1, 2, 2), (MIG, MIG, MIG)]
+ROOMS = [((1, 2, 1), (1, 2, 2)), ((MIG,) * 3,) * 2]
 
 
 def shift_scratch(room):
-    ring = [
-        pltpu.VMEM((MIG, TILE, D), BF16),
-        pltpu.VMEM((sum(room), TILE, D), BF16),
-        pltpu.VMEM((MIG + sum(room), TILE, D), BF16),
-    ]
-    return ring + ring + [
+    rings = []
+    for ways in room:
+        rings += [
+            pltpu.VMEM((MIG, TILE, D), BF16),
+            pltpu.VMEM((sum(ways), TILE, D), BF16),
+            pltpu.VMEM((MIG + sum(ways), TILE, D), BF16),
+        ]
+    return rings + [
         pltpu.VMEM((2, MIG, TILE, D), BF16),
         pltpu.SemaphoreType.DMA((3, 2, 3)),
     ]
@@ -258,7 +260,8 @@
     crowded = jnp.zeros(axes.shape[:-1], jnp.bool_)
     for way, step in enumerate((1, SIDE - 1, 2)):
         count = sum((axes[..., j] == step).astype(jnp.int32) for j in range(MIG))
-        crowded = crowded | (count > ROOMS[0][way])
+        most = [[[[ways[way]]]] for ways in ROOMS[0]]
+        crowded = crowded | (count > jnp.array(most, jnp.int32))
     return ~jnp.any(crowded)
 
 
@@ -298,23 +301,28 @@
     take.wait()
     share.wait()
 
-    def gather(p):
-        first = asked[p, 0, me]
-        other = asked[p, 0, NDOM + here.chip]
-        stage[p, pl.ds(0, TILE)] = feat[core * CL + jnp.maximum(first, 0)]
-        stage[p, pl.ds(TILE, HALF)] = feat[
-            jnp.maximum(other, 0), pl.ds(pl.multiple_of(core * HALF, HALF), HALF)
-        ]
-
-    loop(0, NDOM, gather)
+    def gather_first(low):
+        def one(p):
+            rows = pl.ds(low, HALF)
+            stage[p, rows] = feat[core * CL + jnp.maximum(asked[p, 0, me], 0), rows]
+
+        loop(0, NDOM, one)
+
+    def gather_other(p):
+        other = jnp.maximum(asked[p, 0, NDOM + here.chip], 0)
+        stage[p, pl.ds(TILE, HALF)] = feat[other, pl.ds(pl.multiple_of(core * HALF, HALF), HALF)]
+
+    tiles = Exchange(here, stage, recv_ref, tile_sems.at[0], tile_sems.at[1], 0, WIDE)
+    gather_first(0)
+    tiles.start(0, 4)
+    gather_first(HALF)
+    shift.turn()
+    tiles.start(4, 8)
+    loop(0, NDOM, gather_other)
     keep = pltpu.make_async_copy(
         stage.at[me], recv_ref.at[me, pl.ds(0, WIDE)], local_sems.at[5]
     )
     keep.start()
-    tiles = Exchange(here, stage, recv_ref, tile_sems.at[0], tile_sems.at[1], 0, WIDE)
-    tiles.start(0, 4)
-    shift.turn()
-    tiles.start(4, 8)
     shift.start_lane()
     tiles.start(8, WIDE // CHUNK)
     keep.wait()
@@ -473,7 +481,7 @@
 
     def near(n):
         e = order_ref[n]
-        part = dot_tn(adj[e // KL, e % KL], gm[e // KL]).astype(BF16)
+        part = dot_tn(adj[e % CL, e // CL], gm[e % CL]).astype(BF16)
         running[n + 1] = running[n] + part.astype(F32)
 
     loop(0, NEAR // 2, near)
@@ -692,11 +700,14 @@
 ):
     parts = 2 * KH * GROUP
 
+    def block(n):
+        return block_ref[(n % 2) * CL * KH + (n // 2 % KH) * CL + n // (2 * KH)]
+
     def copy_halo(n):
-        return pltpu.make_async_copy(recv_ref.at[block_ref[n]], halo.at[n], halo_sem.at[n])
+        return pltpu.make_async_copy(recv_ref.at[block(n)], halo.at[n], halo_sem.at[n])
 
     def copy_back(n):
-        return pltpu.make_async_copy(grads.at[n], back_ref.at[block_ref[n]], back_sem.at[n])
+        return pltpu.make_async_copy(grads.at[n], back_ref.at[block(n)], back_sem.at[n])
 
     def group(g):
         return pl.ds(g * GROUP, GROUP)
@@ -738,7 +749,7 @@
             tiles = jnp.concatenate([adj[slot, k] for k in range(KL + KH)], axis=1)
             total = jnp.sum(tiles.astype(F32), axis=1, keepdims=True)
             scale[rows] = jnp.broadcast_to(1.0 / (1.0 + total), (TILE, D))
-            near = [home[src_ref[slot * KL + k]] for k in range(KL)]
+            near = [home[src_ref[k * CL + slot]] for k in range(KL)]
             far = halo[pl.ds(slot * 2 * KH, 2 * KH)].reshape(KH * TILE, D)
             agg = mine.astype(F32) + dot_nn(tiles, jnp.concatenate(near + [far], axis=0))
             mean[slot] = (agg * scale[rows]).astype(BF16)
@@ -868,7 +879,7 @@
             chunk(q, n).wait()
         for n in range(FOUR):
             c = q * FOUR + n
-            first, asked = table_ref[c, me], table_ref[c, NDOM + chip]
+            first, asked = table_ref[c, 0, me], table_ref[c, 0, NDOM + chip]
             other = lax.rem(asked, CL)
 
             @pl.when(first >= 0)
@@ -883,7 +894,7 @@
                 acc[other, rows] += passed[c].astype(F32)
 
             if extra_ref is not None:
-                fourth = table_ref[c, NDOM + CHIPS + chip]
+                fourth = table_ref[c, 0, NDOM + CHIPS + chip]
 
                 @pl.when(jnp.logical_and(fourth >= 0, core == 1))
                 def _():
@@ -962,7 +973,7 @@
         fourth, UNITS * owner + 3, jnp.where(second, 2 * UNITS * chip + 2, UNITS * owner)
     )
     high = jnp.where(second & ~fourth, low + UNITS, low + 1)
-    return row, jnp.stack([low, high], axis=1).reshape(-1)
+    return row, jnp.concatenate([low, high])
 
 
 def sorted_near(src):
@@ -986,9 +997,9 @@
     chip = me // 2
     home = features[0].reshape(CL, TILE, D)
     cot = cotangent[0].reshape(CL, TILE, D)
-    src = local_source.reshape(-1)
+    src = local_source.T.reshape(-1)
     bias = out_bias.reshape(1, D)
-    row, blocks = requests(halo_owner.reshape(-1), halo_local.reshape(-1))
+    row, blocks = requests(halo_owner.T.reshape(-1), halo_local.T.reshape(-1))
     offset = (cluster_plan[OWN:] // CL - me + NDOM) % NDOM
     few = few_ways(offset)
     recv, tables, moved = lax.cond(
@@ -999,12 +1010,13 @@
         row.reshape(1, 128),
         home,
     )
-    asked = tables[:, 0, :]
     order = sorted_near(src)
 
     def rest_of(extra, room, recv, moved):
         if extra:
-            more = lax.dynamic_slice(asked, (0, NDOM + CHIPS + chip), (NDOM, 1)).reshape(-1)
+            more = lax.dynamic_slice(
+                tables, (0, 0, NDOM + CHIPS + chip), (NDOM, 1, 1)
+            ).reshape(-1)
             recv = fourth_forward(more, home, recv)
         new, gp, mean, gm, tail, back = middle(
             blocks, src, recv.reshape(NDOM * UNITS, HALF, D), home, moved, adjacency, cot,
@@ -1015,9 +1027,9 @@
             room, cluster_plan, order, back, tail, gp, gm, mean, home, moved, adjacency, w_self
         )
         got = fourth_backward(back) if extra else None
-        return new, *finish(asked, acc, returned, ret, passed, got, dw, db)
-
-    extra = jnp.any(asked[:, NDOM + CHIPS : NDOM + 2 * CHIPS] >= 0)
+        return new, *finish(tables, acc, returned, ret, passed, got, dw, db)
+
+    extra = jnp.any(tables[:, :, NDOM + CHIPS : NDOM + 2 * CHIPS] >= 0)
     new, grad, dws, dwn, db = lax.switch(
         2 * extra.astype(jnp.int32) + 1 - few.astype(jnp.int32),
         [functools.partial(rest_of, more, room) for more in (False, True) for room in ROOMS],

time: 258 us -> 250 us (0.969)
  the two profiles are of different devices: /device:TPU:3 before, /device:TPU:1 now
where the time goes in v3:
time: 250 us; the launch traced here: 247 us
  Pallas kernels  220 us (88%)
  loops' own time  17 us (7%)
  other arithmetic  4.23 us (2%)
  between operations  3.18 us (1%)
    pallas_call x1, Pallas kernels, exchange_backward(): pl.pallas_call(functools.partial(backward_kernel, room), out_shape=[jax.S...  98.6 us
    pallas_call x1, Pallas kernels, exchange_forward(): pl.pallas_call(functools.partial(forward_kernel, room), out_shape=[jax.Sh...  96.9 us
    another operation x1, loops' own time, body(): lax.switch(2 * extra.astype(jnp.int32) + 1 - few.astype(jnp.int32), [func...  17 us
    pallas_call x1, Pallas kernels, middle(): pl.pallas_call(middle_kernel, out_shape=[tiles, tiles, tiles, tiles, jax....  15.3 us
    pallas_call x1, Pallas kernels, finish(): pl.pallas_call(final_kernel, out_shape=[jax.ShapeDtypeStruct((CL, TILE, D...  9.57 us

profile of v3, /device:TPU:1, one launch (start us, length us, event | category | flops | bytes accessed | tf_op | source)
XLA Modules:
  0.0 246.5 jit_solution(4918486828937333063)
XLA Ops:
  0.6 0.7 broadcast_subtract_fusion
  1.4 0.1 select_shift-right-arithmetic_fusion
  1.5 0.1 fusion.13
  1.5 0.1 add_and_fusion
  1.7 0.1 and_select_fusion
  1.8 1.4 fusion.4
  3.8 0.8 eq.132
  4.6 0.2 fusion.3
  4.8 0.2 and_reduce_fusion
  5.0 0.8 reshape.315
  5.7 0.1 select_reduce_fusion.1
  5.9 96.9 %conditional.2 = (s32[32,1,128]{2,1,0:T(1,128)S(1)}, bf16[32,320,512]{2,1,0:T(8,128)(2,1)}, bf16[3,128,512]{2,1,0:T(8,128)(2,1)S(1)}) conditional(s32[]{:T(128)} %convert_element_type.56, (s32[16]{0:T(128)}, s32[1,128]{1,0:T(1,128)S(1)}, bf16[16,128,512]{2,1,0:T(8,128)(2,1)}) %tuple.67, (s32[16]{0:T(128)}, s32[1,128]{1,0:T(1,128)S(1)}, ...), branch_computations={%region_4.5_spmd.clone, %region_5.6_spmd.clone} | conditional | bytes 24 | solution.py:1005
  5.9 96.9 %branch_1_fun.8 = (bf16[32,320,512]{2,1,0:T(8,128)(2,1)}, s32[32,1,128]{2,1,0:T(1,128)S(1)}, bf16[3,128,512]{2,1,0:T(8,128)(2,1)S(1)}) custom-call(s32[16]{0:T(128)} %get-tuple-element.430.plan_ref, s32[1,128]{1,0:T(1,128)S(1)} %get-tuple-element.431.row_ref, bf16[16,128,512]{2,1,0:T(8,128)(2,1)} %get-tuple-element.432.home_ref), custom_call_target="tpu_custom_call" | custom-call | tf_op jit(solution)/shard_map/cond/branch_1_fun/pallas_call | solution.py:335
  102.8 0.7 compare_reduce_fusion
  104.2 0.1 pad_add_fusion.1
  104.3 0.1 reshape.316
  104.3 0.1 convert_reduce_fusion.1
  104.5 0.2 convert_reduce_fusion
  104.6 0.1 select_reduce_fusion
  104.8 0.1 pad_add_fusion.2
  104.9 140.5 %conditional.3 = (bf16[16,128,512]{2,1,0:T(8,128)(2,1)}, bf16[16,128,512]{2,1,0:T(8,128)(2,1)}, f32[512,512]{1,0:T(8,128)}, f32[512,512]{1,0:T(8,128)}, f32[1,512]{1,0:T(1,128)}) conditional(s32[]{:T(128)} %clamp.3, (bf16[32,320,512]{2,1,0:T(8,128)(2,1)}, s32[64]{0:T(128)S(1)}, s32[48]{0:T(128)S(1)}, ...), branch_computations={%region_10.11_spmd, %region_11.12_spmd, %region_12.13_spmd, %regio... | conditional | flops 19 | bytes 8389416 | solution.py:1033
  105.5 15.3 %branch_0_fun.5 = (bf16[16,128,512]{2,1,0:T(8,128)(2,1)}, bf16[16,128,512]{2,1,0:T(8,128)(2,1)}, bf16[16,128,512]{2,1,0:T(8,128)(2,1)}, bf16[16,128,512]{2,1,0:T...) custom-call(s32[64]{0:T(128)S(1)} %get-tuple-element.276.block_ref, ...), custom_call_target="tpu_custom_call" | custom-call | tf_op jit(solution)/shard_map/cond/branch_0_fun/pallas_call | solution.py:805
  120.8 98.6 %branch_0_fun.6 = (bf16[32,192,512]{2,1,0:T(8,128)(2,1)}, bf16[32,64,512]{2,1,0:T(8,128)(2,1)}, bf16[3,128,512]{2,1,0:T(8,128)(2,1)}, f32[16,128,512]{2,1,0:T(8,...) custom-call(s32[16]{0:T(128)S(1)} %copy-done.7, s32[65]{0:T(128)S(1)} %get-tuple-element.289.order_ref, ...), custom_call_target="tpu_custom_call" | custom-call | tf_op jit(solution)/shard_map/cond/branch_0_fun/pallas_call | solution.py:550
  219.4 9.6 %branch_0_fun.7 = (bf16[16,128,512]{2,1,0:T(8,128)(2,1)}, f32[512,512]{1,0:T(8,128)}, f32[512,512]{1,0:T(8,128)}, f32[1,512]{1,0:T(1,128)}) custom-call(s32[32,1,128]{2,1,0:T(1,128)S(1)} %get-tuple-element.287.table_ref, f32[16,128,512]{2,1,0:T(8,128)} %get-tuple-element.295.acc_ref, bf16[3,128,512]{2,1,0:T(8,128)(2,1)} %get-tuple-element.296.moved_ref, ...), custom_call_target="tpu_custom_call" | custom-call | tf_op jit(solution)/shard_map/cond/branch_0_fun/pallas_call | solution.py:931
  (18 shorter events, 0.2 us)
Async XLA Ops:
  5.8 98.4 %copy-start.11 = (s32[16,3]{0,1:T(4,128)S(1)}, s32[16,3]{0,1:T(4,128)}, u32[]{:S(2)}) copy-start(s32[16,3]{0,1:T(4,128)} %param.24) | copy-start | bytes 580
  5.9 99.0 %copy-start.4 = (bf16[512,512]{1,0:T(8,128)(2,1)S(1)}, bf16[512,512]{1,0:T(8,128)(2,1)}, u32[]{:S(2)}) copy-start(bf16[512,512]{1,0:T(8,128)(2,1)} %param.20) | copy-start | bytes 1572868
  5.9 99.0 %copy-start.5 = (bf16[512,512]{1,0:T(8,128)(2,1)S(1)}, bf16[512,512]{1,0:T(8,128)(2,1)}, u32[]{:S(2)}) copy-start(bf16[512,512]{1,0:T(8,128)(2,1)} %param.21) | copy-start | bytes 1572868
  5.9 99.0 %copy-start.6 = (f32[512]{0:T(512)S(1)}, f32[512]{0:T(512)}, u32[]{:S(2)}) copy-start(f32[512]{0:T(512)} %param.22) | copy-start | bytes 6148
  105.5 15.3 %copy-start = (bf16[16,128,512]{2,1,0:T(8,128)(2,1)S(1)}, bf16[16,128,512]{2,1,0:T(8,128)(2,1)}, u32[]{:S(2)}) copy-start(bf16[16,128,512]{2,1,0:T(8,128)(2,1)} %get-tuple-element.279.home_ref) | copy-start | bytes 6291460 | tf_op jit(solution)/shard_map/cond
  105.5 15.3 %copy-start.7 = (s32[16]{0:T(128)S(1)}, s32[16]{0:T(128)}, u32[]{:S(2)}) copy-start(s32[16]{0:T(128)} %get-tuple-element.288.plan_ref) | copy-start | bytes 196 | tf_op jit(solution)/shard_map/cond
